TPU v7x, 32 devices: a whole 2x2x4 slice. The times are simulated.
32 devices in a mesh: seq: 8 (over z, y), tp: 4 (over x, core).
Axes of the slice: x: 2, y: 2, z: 4, core: 2. Of those that a mesh axis runs over, the one named last changes fastest.
Arguments:
- layer_input: bfloat16 [8, 640, 768], P('seq', 'tp'), may hold values from -6 to 6
- cotangent: bfloat16 [8, 640, 768], P('seq', 'tp'), may hold values from -6 to 6
- seq_lengths: int32 [32], replicated, may hold values from 64 to 512, as said below
- seq_group: int32 [32], replicated, may hold values from 0 to 7, as said below
- norm1_gain: float32 [768], replicated, may hold values from 0.5 to 1.5
- w_qkv: float32 [3, 768, 768], replicated, may hold values from -0.21875 to 0.21875
- mix_logits: float32 [12, 12], replicated, may hold values from -3 to 3
- mix_weights: float32 [12, 12], replicated, may hold values from -1.75 to 1.75
- w_attn_out: float32 [768, 768], replicated, may hold values from -1 to 1
- norm2_gain: float32 [768], replicated, may hold values from 0.5 to 1.5
- w_up: float32 [768, 3072], P(None, 'tp'), may hold values from -0.21875 to 0.21875
- w_down: float32 [3072, 768], P('tp'), may hold values from -0.109375 to 0.109375
Outputs:
- block_out: bfloat16 [8, 640, 768], P('seq', 'tp')
- input_grad: float32 [8, 640, 768], P('seq', 'tp')
- grad_norm1: float32 [768], replicated
- grad_qkv: float32 [3, 768, 768], replicated
- grad_mix_logits: float32 [12, 12], replicated
- grad_mix_weights: float32 [12, 12], replicated
- grad_attn_out: float32 [768, 768], replicated
- grad_norm2: float32 [768], replicated
- grad_up: float32 [768, 3072], P(None, 'tp')
- grad_down: float32 [3072, 768], P('tp')
- qkv_rows: float32 [3, 768], replicated
- qkv_cols: float32 [3, 768], replicated
- out_rows: float32 [768], replicated
- out_cols: float32 [768], replicated
- up_rows: float32 [768], replicated
- up_cols: float32 [3072], P('tp')
- down_rows: float32 [3072], P('tp')
- down_cols: float32 [768], replicated
- new_qkv: float32 [3, 768, 768], replicated
- new_attn_out: float32 [768, 768], replicated
- new_up: float32 [768, 3072], P(None, 'tp')
- new_down: float32 [3072, 768], P('tp')
Inputs may be any that keep to these rules, and one draw needn't show every extreme that they name: `seq_lengths`: each entry is 1, 2, 4 or 8 times 64; for every group g the entries k with seq_group[k] = g add up to 640. `seq_group`: every group is named by some entries.
All inputs are finite; a program needn't handle non-finite values.
Results may differ from a plain program's by a relative error of at most 0.012.
The roundings to bfloat16 on the way count: a program that leaves them out, or rounds other values in their place, can miss the bound.
Values may be sent and summed in bfloat16 or wider, within the bound.
No kernel may reach another device: no remote copies, remote signals or barrier semaphores. Data moves between devices by JAX's collectives and lax.ppermute only.
A program may use at most 384 MiB of HBM per device.

v0:
```python
import jax
import jax.numpy as jnp
from jax import lax
from jax.sharding import PartitionSpec as P

EPS = 1e-06
TINY = 1e-30
STEP = 0.04
HIGH = lax.Precision.HIGHEST


def group_rows(lengths, owners, group_id, shards, tok_dev):
    owned = owners == group_id
    quarter = jnp.where(owned, lengths // shards, 0)
    entry_ids = jnp.arange(lengths.shape[0], dtype=jnp.int32)
    earlier = entry_ids[None, :] < entry_ids[:, None]
    offset = jnp.sum(jnp.where(earlier, quarter[None, :], 0), axis=1)
    row_ids = jnp.arange(tok_dev, dtype=jnp.int32)
    inside = (
        owned[None, :]
        & (offset[None, :] <= row_ids[:, None])
        & (row_ids[:, None] < offset[None, :] + quarter[None, :])
    )
    segment = jnp.sum(jnp.where(inside, entry_ids[None, :], 0), axis=1)
    span_rows = jnp.sum(jnp.where(inside, quarter[None, :], 0), axis=1)
    first_rows = jnp.sum(jnp.where(inside, offset[None, :], 0), axis=1)
    shard_ids = jnp.arange(shards, dtype=jnp.int32)
    position = shard_ids[:, None] * span_rows[None, :] + row_ids[None, :] - first_rows[None, :]
    return (jnp.tile(segment, shards), position.reshape(-1))


def rms_parts(values):
    inv_scale = lax.rsqrt(jnp.mean(values * values, -1, keepdims=True) + EPS)
    return (values * inv_scale, inv_scale)


def rms_back(grad_out, normed, inv_scale, gain):
    grad_normed = grad_out * gain
    grad_in = inv_scale * (grad_normed - normed * jnp.mean(grad_normed * normed, -1, keepdims=True))
    return (grad_in, jnp.sum(grad_out * normed, 0))


def gelu_tanh(values):
    return jax.nn.gelu(values, approximate=True)


def mix_heads(mix_table, stacked):
    return jnp.einsum("gh,gqk->hqk", mix_table, stacked, precision=HIGH)


def unmix_heads(mix_table, stacked):
    return jnp.einsum("gh,hqk->gqk", mix_table, stacked, precision=HIGH)


def pair_total(first_stack, second_stack):
    return jnp.einsum("gqk,hqk->gh", first_stack, second_stack, precision=HIGH)


def scores(queries, key_rows, logit_mix, query_seg, query_pos, key_seg, key_pos):
    score_scale = queries.shape[-1] ** (-0.5)
    logits = (
        jnp.einsum("qhd,khd->hqk", queries, key_rows, preferred_element_type=jnp.float32)
        * score_scale
    )
    mixed_logits = mix_heads(logit_mix, logits)
    visible = (query_seg[:, None] == key_seg[None, :]) & (key_pos[None, :] <= query_pos[:, None])
    return (logits, jnp.where(visible[None], mixed_logits, -jnp.inf))


def attend(
    queries, key_rows, values, logit_mix, weight_mix, query_seg, query_pos, key_seg, key_pos
):
    logits, masked = scores(queries, key_rows, logit_mix, query_seg, query_pos, key_seg, key_pos)
    row_max = jnp.max(masked, -1, keepdims=True)
    totals = jnp.log(jnp.sum(jnp.exp(masked - row_max), -1, keepdims=True)) + row_max
    soft_probs = jnp.exp(masked - totals)
    weights = mix_heads(weight_mix, soft_probs).astype(jnp.bfloat16)
    return (jnp.einsum("hqk,khd->qhd", weights, values, preferred_element_type=jnp.float32), totals)


def attend_back(
    queries,
    key_rows,
    values,
    logit_mix,
    weight_mix,
    query_seg,
    query_pos,
    key_seg,
    key_pos,
    totals,
    grad_out,
):
    score_scale = queries.shape[-1] ** (-0.5)
    logits, masked = scores(queries, key_rows, logit_mix, query_seg, query_pos, key_seg, key_pos)
    soft_probs = jnp.exp(masked - totals)
    weights = mix_heads(weight_mix, soft_probs).astype(jnp.bfloat16)
    grad_weights = jnp.einsum("qhd,khd->hqk", grad_out, values, preferred_element_type=jnp.float32)
    grad_weight_mix = pair_total(soft_probs, grad_weights)
    grad_probs = unmix_heads(weight_mix, grad_weights)
    grad_mixed = soft_probs * (grad_probs - jnp.sum(soft_probs * grad_probs, -1, keepdims=True))
    grad_logit_mix = pair_total(logits, grad_mixed)
    grad_logits = unmix_heads(logit_mix, grad_mixed).astype(jnp.bfloat16)
    grad_query = (
        jnp.einsum("hqk,khd->qhd", grad_logits, key_rows, preferred_element_type=jnp.float32)
        * score_scale
    )
    grad_key = (
        jnp.einsum("hqk,qhd->khd", grad_logits, queries, preferred_element_type=jnp.float32)
        * score_scale
    )
    grad_value = jnp.einsum("hqk,qhd->khd", weights, grad_out, preferred_element_type=jnp.float32)
    return (grad_query, grad_key, grad_value, grad_logit_mix, grad_weight_mix)


def factored(weight, gradient):
    squares = gradient * gradient + TINY
    row_means = jnp.mean(squares, -1)
    col_means = jnp.mean(squares, -2)
    row_scale = jnp.mean(row_means, -1, keepdims=True)
    second = row_means[..., :, None] * col_means[..., None, :] / row_scale[..., None]
    return (row_means, col_means, weight - STEP * gradient * lax.rsqrt(second))


def per_device(
    layer_input,
    cotangent,
    seq_lengths,
    seq_group,
    norm1_gain,
    w_qkv,
    mix_logits,
    mix_weights,
    w_attn_out,
    norm2_gain,
    w_up,
    w_down,
):
    shards = lax.axis_size("tp")
    shard_id = lax.axis_index("tp")
    group_id = lax.axis_index("seq")
    tok_dev = layer_input.shape[1]
    group_tok = tok_dev * shards
    model_width = layer_input.shape[2]
    head_count = mix_logits.shape[0]
    head_dim = model_width // head_count
    block_rows = group_tok // min(2, group_tok // 1024 + 1)
    segment, position = group_rows(seq_lengths, seq_group, group_id, shards, tok_dev)
    own_start = shard_id * tok_dev
    gathered = lax.all_gather(layer_input, "tp", axis=1, tiled=True)[0]
    inputs = gathered.astype(jnp.float32)
    normed1, inv1 = rms_parts(inputs)
    normed_in = (normed1 * norm1_gain).astype(jnp.bfloat16)
    normed_in_own = lax.dynamic_slice_in_dim(normed_in, own_start, tok_dev)
    normed1_own = lax.dynamic_slice_in_dim(normed1, own_start, tok_dev)
    inv1_own = lax.dynamic_slice_in_dim(inv1, own_start, tok_dev)
    qkv_b = w_qkv.astype(jnp.bfloat16)
    out_b = w_attn_out.astype(jnp.bfloat16)
    up_b = w_up.astype(jnp.bfloat16)
    down_b = w_down.astype(jnp.bfloat16)
    projected = jnp.einsum("nd,ide->ine", normed_in, qkv_b, preferred_element_type=jnp.float32)
    projected = projected.astype(jnp.bfloat16).reshape(3, group_tok, head_count, head_dim)
    block_id = 0
    low_row = block_id * block_rows
    key_end = low_row + block_rows
    head_block, totals = attend(
        projected[0, low_row:key_end],
        projected[1, :key_end],
        projected[2, :key_end],
        mix_logits,
        mix_weights,
        segment,
        position,
        segment,
        position,
    )
    totals_list = [totals]
    attn_rows = head_block.reshape(group_tok, model_width).astype(jnp.bfloat16)
    residual = inputs + jnp.dot(attn_rows, out_b, preferred_element_type=jnp.float32)
    normed2, inv2 = rms_parts(residual)
    normed_mid = (normed2 * norm2_gain).astype(jnp.bfloat16)
    resid_own = lax.dynamic_slice_in_dim(residual, own_start, tok_dev)
    up_pre = jnp.dot(normed_mid, up_b, preferred_element_type=jnp.float32)
    activated, gelu_back = jax.vjp(gelu_tanh, up_pre)
    act_b = activated.astype(jnp.bfloat16)
    branch_own = lax.psum_scatter(
        jnp.dot(act_b, down_b, preferred_element_type=jnp.float32),
        "tp",
        scatter_dimension=0,
        tiled=True,
    )
    block_out = (resid_own + branch_own).astype(jnp.bfloat16)[None]
    cot_all = lax.all_gather(cotangent, "tp", axis=1, tiled=True)[0]
    grad_down = jnp.einsum("nf,nd->fd", act_b, cot_all, preferred_element_type=jnp.float32)
    grad_act = jnp.einsum("nd,fd->nf", cot_all, down_b, preferred_element_type=jnp.float32)
    grad_up_in = gelu_back(grad_act)[0].astype(jnp.bfloat16)
    grad_up = jnp.einsum("nd,nf->df", normed_mid, grad_up_in, preferred_element_type=jnp.float32)
    grad_mid = lax.psum(
        jnp.einsum("nf,df->nd", grad_up_in, up_b, preferred_element_type=jnp.float32), "tp"
    )
    grad_res_norm, ignored = rms_back(grad_mid, normed2, inv2, norm2_gain)
    grad_norm2 = jnp.sum(
        lax.dynamic_slice_in_dim(grad_mid, own_start, tok_dev)
        * lax.dynamic_slice_in_dim(normed2, own_start, tok_dev),
        0,
    )
    grad_res = cot_all.astype(jnp.float32) + grad_res_norm
    grad_res_b = grad_res.astype(jnp.bfloat16)
    grad_res_own_b = lax.dynamic_slice_in_dim(grad_res_b, own_start, tok_dev)
    attn_own = lax.dynamic_slice_in_dim(attn_rows, own_start, tok_dev)
    grad_attn_out = jnp.einsum(
        "nd,ne->de", attn_own, grad_res_own_b, preferred_element_type=jnp.float32
    )
    grad_heads = jnp.einsum("ne,de->nd", grad_res_b, out_b, preferred_element_type=jnp.float32)
    grad_heads = grad_heads.astype(jnp.bfloat16).reshape(group_tok, head_count, head_dim)
    block_id = 0
    low_row = block_id * block_rows
    key_end = low_row + block_rows
    block_grads = attend_back(
        projected[0, low_row:key_end],
        projected[1, :key_end],
        projected[2, :key_end],
        mix_logits,
        mix_weights,
        segment,
        position,
        segment,
        position,
        totals_list[block_id],
        grad_heads,
    )
    grad_query_parts = block_grads[0]
    grad_key_sum = block_grads[1]
    grad_value_sum = block_grads[2]
    logit_mix_sum = block_grads[3]
    weight_mix_sum = block_grads[4]
    logit_mix_sum = logit_mix_sum / shards
    weight_mix_sum = weight_mix_sum / shards
    grad_qkv_b = jnp.stack([grad_query_parts, grad_key_sum, grad_value_sum])
    grad_qkv_b = grad_qkv_b.reshape(3, group_tok, model_width).astype(jnp.bfloat16)
    grad_qkv_own_b = lax.dynamic_slice_in_dim(grad_qkv_b, own_start, tok_dev, 1)
    grad_qkv = jnp.einsum(
        "nd,ine->ide", normed_in_own, grad_qkv_own_b, preferred_element_type=jnp.float32
    )
    grad_in_rows = jnp.einsum(
        "ine,ide->nd", grad_qkv_own_b, qkv_b, preferred_element_type=jnp.float32
    )
    grad_in_norm, grad_norm1 = rms_back(grad_in_rows, normed1_own, inv1_own, norm1_gain)
    input_grad = lax.dynamic_slice_in_dim(grad_res, own_start, tok_dev) + grad_in_norm
    attn_sums = lax.psum(
        (grad_norm1, grad_qkv, logit_mix_sum, weight_mix_sum, grad_attn_out, grad_norm2),
        ("seq", "tp"),
    )
    ffn_sums = lax.psum((grad_up, grad_down), "seq")
    grad_norm1, grad_qkv, grad_mix_logits, grad_mix_weights, grad_attn_out, grad_norm2 = attn_sums
    grad_up, grad_down = ffn_sums
    qkv_rows, qkv_cols, new_qkv = factored(w_qkv, grad_qkv)
    out_rows, out_cols, new_attn_out = factored(w_attn_out, grad_attn_out)
    full_hidden = w_up.shape[1] * shards
    squares_up = grad_up * grad_up + TINY
    squares_down = grad_down * grad_down + TINY
    down_rows_mean = jnp.mean(squares_down, 1)
    up_total, down_total = lax.psum((jnp.sum(squares_up, 1), jnp.sum(squares_down, 0)), "tp")
    up_rows = up_total / full_hidden
    up_cols = jnp.mean(squares_up, 0)
    up_scale = jnp.mean(up_rows, -1, keepdims=True)
    new_up = w_up - STEP * grad_up * lax.rsqrt(
        up_rows[:, None] * up_cols[None, :] / up_scale[..., None]
    )
    down_cols = down_total / full_hidden
    down_scale = jnp.mean(down_cols)
    new_down = w_down - STEP * grad_down * lax.rsqrt(
        down_rows_mean[:, None] * down_cols[None, :] / down_scale
    )
    return (
        block_out,
        input_grad[None],
        grad_norm1,
        grad_qkv,
        grad_mix_logits,
        grad_mix_weights,
        grad_attn_out,
        grad_norm2,
        grad_up,
        grad_down,
        qkv_rows,
        qkv_cols,
        out_rows,
        out_cols,
        up_rows,
        up_cols,
        down_rows_mean,
        down_cols,
        new_qkv,
        new_attn_out,
        new_up,
        new_down,
    )


def solution(mesh):
    return jax.shard_map(
        per_device,
        mesh=mesh,
        in_specs=(
            P("seq", "tp", None),
            P("seq", "tp", None),
            P(),
            P(),
            P(),
            P(),
            P(),
            P(),
            P(),
            P(),
            P(None, "tp"),
            P("tp", None),
        ),
        out_specs=(
            P("seq", "tp", None),
            P("seq", "tp", None),
            P(),
            P(),
            P(),
            P(),
            P(),
            P(),
            P(None, "tp"),
            P("tp", None),
            P(),
            P(),
            P(),
            P(),
            P(),
            P("tp"),
            P("tp"),
            P(),
            P(),
            P(),
            P(None, "tp"),
            P("tp", None),
        ),
        check_vma=False,
    )
```

profile of v0, /device:TPU:0, one launch (start us, length us, event | category | flops | bytes accessed | tf_op | source)
XLA Modules:
  0.0 705.5 jit_solution(8797912714574456082)
XLA Ops:
  7.3 11.3 %all_gather.6 = bf16[1,640,768]{2,1,0:T(8,128)(2,1)S(1)} all-gather(bf16[1,160,768]{2,1,0:T(8,128)(2,1)} %param.12), channel_id=1, replica_groups=mesh['seq'=8,'tp'=4] {'tp'}, dimensions={1}, use_global_device_ids=true | all-gather | bytes 1228800 | tf_op jit(solution)/shard_map/all_gather | solution.py:150
  18.9 2.3 convert_multiply_fusion
  21.1 5.9 convert_bitcast_fusion.2
  27.3 1.3 copy.82
  29.0 0.6 copy.83
  29.7 1.4 copy.84
  31.5 4.0 broadcast_multiply_fusion
  35.5 61.5 %bitcast_reduce_fusion = (f32[12,640]{0,1:T(8,128)S(1)}, f32[640,640,12]{1,2,0:T(8,128)}) fusion(pred[640,640]{1,0:T(8,128)(4,1)S(1)} %compare_and_fusion, f32[12,12]{1,0:T(8,128)S(1)} %copy-done.42, f32[12,640,640]{2,1,0:T(8,128)S(1)} %broadcast_multiply_fusion), kind=kOutput, calls=%fused_computation.14 | convolution fusion | flops 717611520 | bytes 39762496 | tf_op jit(solution)/shard_map/gh,gqk->hqk/dot_general | solution.py:48
  97.0 19.8 %fusion.11 = f32[12,640]{0,1:T(8,128)S(1)} fusion(f32[640,640,12]{1,2,0:T(8,128)} %get-tuple-element.129, f32[12,640]{0,1:T(8,128)S(1)} %get-tuple-element.128, pred[640,640]{1,0:T(8,128)(4,1)S(1)} %compare_and_fusion), kind=kLoop, calls=%fused_computation.16 | loop fusion | flops 14737920 | bytes 20131840 | tf_op jit(solution)/shard_map/reduce_sum | solution.py:75
  116.9 36.5 %convert_bitcast_fusion.1 = bf16[12,640,640]{2,0,1:T(8,128)(2,1)} fusion(f32[640,640,12]{1,2,0:T(8,128)} %get-tuple-element.129, f32[12,640]{0,1:T(8,128)S(1)} %log_add_fusion, pred[640,640]{1,0:T(8,128)(4,1)S(1)} %compare_and_fusion, f32[12,12]{1,0:T(8,128)S(1)} %copy-done), kind=kOutput, calls=%fused_computation.19 | convolution fusion | flops 722534400 | bytes 29932096 | tf_op jit(solution)/shard_map/gh,gqk->hqk/dot_general | solution.py:48
  153.5 8.7 %fusion.51 = bf16[12,64,640]{2,1,0:T(8,128)(2,1)S(1)} fusion(bf16[640,12,64]{0,2,1:T(8,128)(2,1)S(1)} %bitcast.144, bf16[12,640,640]{2,0,1:T(8,128)(2,1)} %convert_bitcast_fusion.1), kind=kOutput, calls=%fused_computation.76 | convolution fusion | flops 629637120 | bytes 11796480 | tf_op jit(solution)/shard_map/hqk,khd->qhd/dot_general | solution.py:78
  162.2 1.1 multiply_reduce_fusion.1
  163.4 9.9 %all_gather.7 = bf16[1,640,768]{2,1,0:T(8,128)(2,1)S(1)} all-gather(bf16[1,160,768]{2,1,0:T(8,128)(2,1)S(1)} %copy-done.37), channel_id=1, replica_groups=mesh['seq'=8,'tp'=4] {'tp'}, dimensions={1}, use_global_device_ids=true | all-gather | bytes 1228800 | tf_op jit(solution)/shard_map/all_gather | solution.py:193
  173.6 0.9 fusion.94
  174.9 1.1 copy-done.30
  176.1 1.9 fusion.42
  178.0 1.0 copy-done.24
  178.9 2.2 fusion.92
  181.2 4.8 fusion.90
  186.2 4.8 fusion.100
  191.0 2.7 fusion.80
  193.8 20.2 %fusion.145 = f32[12,640,640]{2,0,1:T(8,128)} fusion(f32[640,640,12]{1,2,0:T(8,128)} %get-tuple-element.129, f32[12,640]{0,1:T(8,128)S(1)} %log_add_fusion, pred[640,640]{1,0:T(8,128)(4,1)S(1)} %compare_and_fusion), kind=kLoop, calls=%fused_computation.17.clone.clone.clone.clone.clone.clone.1 | loop fusion | flops 9830400 | bytes 39761920 | tf_op jit(solution)/shard_map/gqk,hqk->gh/dot_general | solution.py:56
  214.0 8.1 %copy.99 = f32[3,768,768]{1,2,0:T(8,128)} copy(f32[3,768,768]{2,1,0:T(8,128)} %param.17) | data formatting | bytes 14155776 | tf_op args[5]
  222.1 0.6 dynamic-slice.3
  222.8 8.7 %all-reduce.8.cloned.1.call-done = f32[640,768]{1,0:T(8,128)} async-done(((f32[640,768]{1,0:T(8,128)}), f32[640,768]{1,0:T(8,128)}) %all-reduce.8.cloned.1.call-update) | async-done | bytes 1966096 | tf_op jit(solution)/shard_map/psum | solution.py:198
  231.5 2.2 multiply_reduce_fusion
  233.9 1.9 fusion.124
  235.7 0.9 copy-done.35
  236.7 1.9 convolution_convert_fusion
  238.6 1.5 copy.89
  240.1 8.3 %fusion.126 = f32[12,640,640]{2,1,0:T(8,128)} fusion(bf16[640,12,64]{0,2,1:T(8,128)(2,1)S(1)} %bitcast.150, bf16[640,12,64]{0,2,1:T(8,128)(2,1)S(1)} %bitcast.145), kind=kOutput, calls=%fused_computation.159 | convolution fusion | flops 629145600 | bytes 21626880 | tf_op jit(solution)/shard_map/qhd,khd->hqk/dot_general | solution.py:98
  248.5 64.0 %fusion.8 = (f32[12,640]{0,1:T(8,128)S(1)}, f32[640,640,12]{1,2,0:T(8,128)}) fusion(f32[12,640]{0,1:T(8,128)S(1)} %log_add_fusion, f32[640,640,12]{1,2,0:T(8,128)} %get-tuple-element.129, pred[640,640]{1,0:T(8,128)(4,1)S(1)} %compare_and_fusion, f32[12,12]{1,0:T(8,128)S(1)} %copy-done, f32[12,640,640]{2,1,0:T(8,128)} %fusion.126), kind=kOutput, calls=%fused_computation.10 | convolution fusion | flops 727441920 | bytes 59454016 | tf_op jit(solution)/shard_map/gh,hqk->gqk/dot_general | solution.py:52
  312.5 37.9 %convert_bitcast_fusion = bf16[12,640,640]{2,0,1:T(8,128)(2,1)} fusion(f32[640,640,12]{1,2,0:T(8,128)} %get-tuple-element.133, f32[12,640]{0,1:T(8,128)S(1)} %get-tuple-element.132, f32[12,640]{0,1:T(8,128)S(1)} %log_add_fusion, f32[640,640,12]{1,2,0:T(8,128)} %get-tuple-element.129, pred[640,640]{1,0:T(8,128)(4,1)S(1)} %compare_and_fusion, ...), kind=kOutput, calls=%fused_computation.18 | convolution fusion | flops 732364800 | bytes 49623616 | tf_op jit(solution)/shard_map/gh,hqk->gqk/dot_general | solution.py:52
  350.4 28.3 %fusion.147 = f32[12,640,640]{2,0,1:T(8,128)} fusion(f32[640,640,12]{1,2,0:T(8,128)} %get-tuple-element.133, f32[12,640]{0,1:T(8,128)S(1)} %get-tuple-element.132, f32[12,640]{0,1:T(8,128)S(1)} %log_add_fusion, f32[640,640,12]{1,2,0:T(8,128)} %get-tuple-element.129, pred[640,640]{1,0:T(8,128)(4,1)S(1)} %compare_and_fusion), kind=kLoop, calls=%fused_computation.11.clone.clone.clone.clone.clone.clone.1 | loop fusion | flops 19660800 | bytes 59453440 | tf_op jit(solution)/shard_map/gqk,hqk->gh/dot_general | solution.py:56
  378.8 9.6 %multiply_convert_fusion.1 = bf16[12,64,640]{2,1,0:T(8,128)(2,1)} fusion(bf16[640,12,64]{0,2,1:T(8,128)(2,1)S(1)} %bitcast.149, bf16[12,640,640]{2,0,1:T(8,128)(2,1)} %convert_bitcast_fusion), kind=kOutput, calls=%fused_computation.65 | convolution fusion | flops 630128640 | bytes 11796480 | tf_op jit(solution)/shard_map/hqk,khd->qhd/dot_general | solution.py:105
  388.3 9.4 %multiply_convert_fusion = bf16[12,64,640]{2,1,0:T(8,128)(2,1)} fusion(bf16[640,12,64]{0,2,1:T(8,128)(2,1)S(1)} %bitcast.147, bf16[12,640,640]{2,0,1:T(8,128)(2,1)} %convert_bitcast_fusion), kind=kOutput, calls=%fused_computation.64 | convolution fusion | flops 630128640 | bytes 11796480 | tf_op jit(solution)/shard_map/hqk,qhd->khd/dot_general | solution.py:109
  397.7 0.6 copy.94
  398.4 1.9 copy.95
  400.3 9.6 %fusion.54 = bf16[12,64,640]{2,1,0:T(8,128)(2,1)} fusion(bf16[640,12,64]{0,2,1:T(8,128)(2,1)S(1)} %bitcast.151, bf16[12,640,640]{2,0,1:T(8,128)(2,1)} %convert_bitcast_fusion.1), kind=kOutput, calls=%fused_computation.77 | convolution fusion | flops 629637120 | bytes 11796480 | tf_op jit(solution)/shard_map/hqk,qhd->khd/dot_general | solution.py:112
  410.0 2.0 copy.96
  412.0 3.4 fusion.98
  415.4 5.1 convolution_bitcast_fusion
  420.4 46.8 %fusion.75 = f32[12,12]{1,0:T(8,128)S(1)} fusion(f32[12,640,640]{2,1,0:T(8,128)} %copy-done.2, f32[12,640,640]{2,0,1:T(8,128)} %fusion.147), kind=kOutput, calls=%fused_computation.83 | convolution fusion | flops 707788928 | bytes 39322176 | tf_op jit(solution)/shard_map/gqk,hqk->gh/dot_general | solution.py:56
  467.4 46.8 %fusion.70 = f32[12,12]{1,0:T(8,128)S(1)} fusion(f32[12,640,640]{2,1,0:T(8,128)} %fusion.126, f32[12,640,640]{2,0,1:T(8,128)} %fusion.145), kind=kOutput, calls=%fused_computation.82 | convolution fusion | flops 707788928 | bytes 39322176 | tf_op jit(solution)/shard_map/gqk,hqk->gh/dot_general | solution.py:56
  514.2 1.3 multiply_reduce_fusion.2
  515.6 2.5 multiply_reduce_fusion.3
  518.1 41.6 %all-reduce = (f32[768]{0:T(1024)}, f32[12,12]{1,0:T(8,128)}, f32[12,12]{1,0:T(8,128)}, f32[768]{0:T(1024)}) all-reduce(f32[768]{0:T(1024)S(1)} %get-tuple-element.90, f32[12,12]{1,0:T(8,128)S(1)} %fusion.75, f32[12,12]{1,0:T(8,128)S(1)} %fusion.70, f32[768]{0:T(1024)S(1)} %multiply_reduce_fusion.2), channel_id=1, replica_groups=mesh['seq'=8,'tp'=4] {'seq','tp'}, use_global_device_ids=true, to_apply=%region_14.15 | all-reduce | flops 1824 | bytes 14592 | tf_op jit(solution)/shard_map/psum | solution.py:250
  559.6 2.1 add_bitcast_fusion
  561.7 1.9 fusion.101
  563.7 2.3 fusion.32
  566.5 7.0 all-reduce.3
  573.5 0.6 fusion.120
  576.1 5.1 multiply_subtract_fusion.1
  581.2 78.0 %all-reduce.10.cloned.1.call-done = (f32[3,768,768]{1,2,0:T(8,128)}, f32[768,768]{1,0:T(8,128)}) async-done(((f32[3,768,768]{1,2,0:T(8,128)}, f32[768,768]{1,0:T(8,128)}), (f32[3,768,768]{1,2,0:T(8,128)}, f32[768,768]{1,0:T(8,128)})) %all-reduce.10.cloned.1.call-update) | async-done | bytes 9437200 | tf_op jit(solution)/shard_map/psum | solution.py:250
  659.2 8.0 %copy.100 = f32[3,768,768]{2,1,0:T(8,128)} copy(f32[3,768,768]{1,2,0:T(8,128)} %get-tuple-element.105) | data formatting | bytes 14155776
  667.3 4.3 fusion.26
  671.6 2.1 fusion.30
  673.9 5.7 multiply_subtract_fusion
  679.6 8.0 %copy.101 = f32[3,768,768]{2,1,0:T(8,128)} copy(f32[3,768,768]{1,2,0:T(8,128)} %multiply_subtract_fusion) | data formatting | bytes 14155776
  688.9 4.5 multiply_subtract_fusion.3
  693.4 1.4 copy.149
  694.8 1.1 copy-done.6
  695.9 1.4 copy.150
  697.3 1.4 copy.151
  (139 shorter events, 4.6 us)
Async XLA Ops:
  7.2 109.7 %copy-start = (f32[12,12]{1,0:T(8,128)S(1)}, f32[12,12]{1,0:T(8,128)}, u32[]{:S(2)}) copy-start(f32[12,12]{1,0:T(8,128)} %param.19) | copy-start | bytes 1732
  7.2 224.3 %all-reduce.8.cloned.1.call-start = ((), (), s32[]{:S(2)}) async-start(), calls=%async_computation.2 | async-start | bytes 3932160 | tf_op jit(solution)/shard_map/psum | solution.py:198
  18.6 2.6 copy-start.10
  21.1 5.9 copy-start.34
  27.0 1.6 copy-start.50
  27.1 1.5 copy-start.51
  29.7 5.8 copy-start.27
  31.4 4.0 copy-start.42
  35.4 61.5 %copy-start.2 = (f32[12,640,640]{2,1,0:T(8,128)}, f32[12,640,640]{2,1,0:T(8,128)S(1)}, u32[]{:S(2)}) copy-start(f32[12,640,640]{2,1,0:T(8,128)S(1)} %broadcast_multiply_fusion) | copy-start | bytes 58982404
  116.9 36.6 %copy-start.25 = (bf16[1,640,768]{1,2,0:T(8,128)(2,1)S(1)}, bf16[1,640,768]{1,2,0:T(8,128)(2,1)}, u32[]{:S(2)}) copy-start(bf16[1,640,768]{1,2,0:T(8,128)(2,1)} %copy.82) | copy-start | bytes 2949124
  153.5 8.7 %copy-start.11 = (bf16[1,640,768]{2,1,0:T(8,128)(2,1)S(1)}, bf16[1,640,768]{2,1,0:T(8,128)(2,1)}, u32[]{:S(2)}) copy-start(bf16[1,640,768]{2,1,0:T(8,128)(2,1)} %copy-done.10) | copy-start | bytes 2949124
  153.5 8.7 %copy-start.13 = (f32[768,768]{1,0:T(8,128)S(1)}, f32[768,768]{1,0:T(8,128)}, u32[]{:S(2)}) copy-start(f32[768,768]{1,0:T(8,128)} %param.20) | copy-start | bytes 7077892
  162.2 1.2 copy-start.33
  162.2 1.2 copy-start.37
  163.3 70.3 %copy-start.4 = (f32[640,768]{1,0:T(8,128)}, f32[640,768]{1,0:T(8,128)S(1)}, u32[]{:S(2)}) copy-start(f32[640,768]{1,0:T(8,128)S(1)} %get-tuple-element.131) | copy-start | bytes 5898244
  163.4 10.1 %copy-start.8 = (f32[768,768]{1,0:T(8,128)S(1)}, f32[768,768]{1,0:T(8,128)}, u32[]{:S(2)}) copy-start(f32[768,768]{1,0:T(8,128)} %param.22) | copy-start | bytes 7077892
  163.4 10.1 %copy-start.38 = (f32[768]{0:T(1024)S(1)}, f32[768]{0:T(1024)}, u32[]{:S(2)}) copy-start(f32[768]{0:T(1024)} %param.21) | copy-start | bytes 9220
  173.3 1.2 copy-start.21
  173.6 1.4 copy-start.9
  173.6 2.5 copy-start.30
  176.1 1.9 copy-start.31
  178.0 1.0 copy-start.24
  181.2 380.5 %reduce-scatter.2.cloned.1.call-start = ((), (), s32[]{:S(2)}) async-start(), calls=%async_computation.1 | async-start | bytes 2457600 | tf_op jit(solution)/shard_map/reduce_scatter | solution.py:186
  186.1 377.6 %all-reduce.12.cloned.1.call-start = ((), (), s32[]{:S(2)}) async-start(), calls=%async_computation.4 | async-start | bytes 9437184 | tf_op jit(solution)/shard_map/psum | solution.py:254
  186.2 4.8 copy-start.22
  186.2 4.8 copy-start.32
  193.8 465.5 %all-reduce.10.cloned.1.call-start = ((), (), s32[]{:S(2)}) async-start(), calls=%async_computation.3 | async-start | bytes 18874368 | tf_op jit(solution)/shard_map/psum | solution.py:250
  231.5 2.2 copy-start.12
  231.5 2.4 copy-start.23
  233.9 2.8 copy-start.14
  235.7 0.9 copy-start.35
  236.7 3.5 copy-start.26
  350.4 28.3 %copy-start.29 = (bf16[1,640,768]{1,2,0:T(8,128)(2,1)S(1)}, bf16[1,640,768]{1,2,0:T(8,128)(2,1)}, u32[]{:S(2)}) copy-start(bf16[1,640,768]{1,2,0:T(8,128)(2,1)} %copy.84) | copy-start | bytes 2949124
  378.8 9.6 %copy-start.28 = (bf16[1,640,768]{1,2,0:T(8,128)(2,1)S(1)}, bf16[1,640,768]{1,2,0:T(8,128)(2,1)}, u32[]{:S(2)}) copy-start(bf16[1,640,768]{1,2,0:T(8,128)(2,1)} %copy-done.27) | copy-start | bytes 2949124
  388.3 9.4 %copy-start.36 = (bf16[12,64,640]{2,1,0:T(8,128)(2,1)S(1)}, bf16[12,64,640]{2,1,0:T(8,128)(2,1)}, u32[]{:S(2)}) copy-start(bf16[12,64,640]{2,1,0:T(8,128)(2,1)} %multiply_convert_fusion.1) | copy-start | bytes 2949124
  398.4 17.0 %copy-start.15 = (bf16[1,640,768]{2,1,0:T(8,128)(2,1)}, bf16[1,640,768]{2,1,0:T(8,128)(2,1)S(1)}, u32[]{:S(2)}) copy-start(bf16[1,640,768]{2,1,0:T(8,128)(2,1)S(1)} %copy.94) | copy-start | bytes 2949124
  400.3 15.0 %copy-start.17 = (bf16[1,640,768]{2,1,0:T(8,128)(2,1)}, bf16[1,640,768]{2,1,0:T(8,128)(2,1)S(1)}, u32[]{:S(2)}) copy-start(bf16[1,640,768]{2,1,0:T(8,128)(2,1)S(1)} %copy.95) | copy-start | bytes 2949124
  411.9 8.5 %copy-start.19 = (bf16[1,640,768]{2,1,0:T(8,128)(2,1)}, bf16[1,640,768]{2,1,0:T(8,128)(2,1)S(1)}, u32[]{:S(2)}) copy-start(bf16[1,640,768]{2,1,0:T(8,128)(2,1)S(1)} %copy.96) | copy-start | bytes 2949124
  467.3 48.2 %slice-start = ((s8[7077888]{0:T(1024)(128)(4,1)}), s8[2883584]{0:T(1024)(128)(4,1)S(1)}, s32[]{:S(2)}) async-start(s8[7077888]{0:T(1024)(128)(4,1)} %bitcast.142), calls=%async_computation.5 | async-start | bytes 5767168
  467.3 48.2 %slice-start.1 = ((s8[7077888]{0:T(1024)(128)(4,1)}), s8[4194304]{0:T(1024)(128)(4,1)S(1)}, s32[]{:S(2)}) async-start(s8[7077888]{0:T(1024)(128)(4,1)} %bitcast.142), calls=%async_computation.6 | async-start | bytes 8388608
  467.3 48.2 %copy-start.16 = (bf16[1,640,768]{2,1,0:T(8,128)(2,1)S(1)}, bf16[1,640,768]{2,1,0:T(8,128)(2,1)}, u32[]{:S(2)}) copy-start(bf16[1,640,768]{2,1,0:T(8,128)(2,1)} %copy-done.15) | copy-start | bytes 2949124
  467.3 48.2 %copy-start.18 = (bf16[1,640,768]{2,1,0:T(8,128)(2,1)S(1)}, bf16[1,640,768]{2,1,0:T(8,128)(2,1)}, u32[]{:S(2)}) copy-start(bf16[1,640,768]{2,1,0:T(8,128)(2,1)} %copy-done.17) | copy-start | bytes 2949124
  467.4 48.2 %copy-start.20 = (bf16[1,640,768]{2,1,0:T(8,128)(2,1)S(1)}, bf16[1,640,768]{2,1,0:T(8,128)(2,1)}, u32[]{:S(2)}) copy-start(bf16[1,640,768]{2,1,0:T(8,128)(2,1)} %copy-done.19) | copy-start | bytes 2949124
  467.4 48.2 %copy-start.41 = (f32[768]{0:T(1024)S(1)}, f32[768]{0:T(1024)}, u32[]{:S(2)}) copy-start(f32[768]{0:T(1024)} %param.16) | copy-start | bytes 9220
  515.6 44.1 %copy-start.49 = (f32[160]{0:T(256)S(1)}, f32[160]{0:T(256)}, u32[]{:S(2)}) copy-start(f32[160]{0:T(256)} %dynamic-slice.3) | copy-start | bytes 1924
  563.7 2.4 copy-start.5
  574.1 7.1 copy-start.43
  575.4 5.8 copy-start.44
  576.1 5.1 copy-start.45
  576.1 5.1 copy-start.46
  667.3 6.6 copy-start.3
  673.9 5.7 copy-start.39
  673.9 5.7 copy-start.40
  688.3 5.1 copy-start.47
  688.3 5.1 copy-start.48
  688.9 4.5 copy-start.7
  693.4 2.5 copy-start.6
  695.9 2.8 copy-start.1
Sparse Core Ops, SparseCore 0:
  181.3 50.1 all-reduce.7
  234.6 30.6 reduce-scatter.1
  270.0 170.0 all-reduce.11
  467.4 191.7 all-reduce.9
where the time goes:
time: 712 us; the launch traced here: 705 us
  matrix products  381 us (54%)
  other arithmetic  107 us (15%)
  waiting for transfers between devices  86.8 us (12%)
  blocking collectives  69.8 us (10%)
  local copies, waits for them, and re-layouts  44 us (6%)
  between operations  16.7 us (2%)
    dot_general x2, matrix products, unmix_heads(): return jnp.einsum('gh,hqk->gqk', mix_table, stacked, precision=HIGH)  102 us
    dot_general x2, matrix products, mix_heads(): return jnp.einsum('gh,gqk->hqk', mix_table, stacked, precision=HIGH)  98.1 us
    dot_general x2, matrix products, pair_total(): return jnp.einsum('gqk,hqk->gh', first_stack, second_stack, precision=HIGH)  93.7 us
    psum x1, waiting for transfers between devices, per_device(): lax.psum((grad_norm1, grad_qkv, logit_mix_sum, weight_mix_sum, grad_attn_...  78 us
    dot_general x2, other arithmetic, pair_total(): return jnp.einsum('gqk,hqk->gh', first_stack, second_stack, precision=HIGH)  48.5 us
    psum x1, blocking collectives, per_device(): lax.psum((grad_norm1, grad_qkv, logit_mix_sum, weight_mix_sum, grad_attn_...  41.6 us
    unnamed x114, local copies, waits for them, and re-layouts  33.6 us
    reduce_sum x1, other arithmetic, attend(): jnp.sum(jnp.exp(masked - row_max), -1, keepdims=True)  19.8 us
  transfers between devices with their start and end apart: 4, of which 2 were waited for; matrix products, arithmetic and copies ran while one was open for 48% of the time, Pallas kernels for 0%

commit v1 on v0

v1 whole, which is shorter than its diff:
```python
import functools

import jax
import jax.numpy as jnp
from jax import lax
from jax.experimental import pallas as pl
from jax.experimental.pallas import tpu as pltpu
from jax.sharding import PartitionSpec as P

EPS = 1e-06
TINY = 1e-30
STEP = 0.04
F32 = jnp.float32
BF16 = jnp.bfloat16
HEAD_BLOCK = 6
VMEM_LIMIT = 48 * 1024 * 1024


def cost(micros):
    return pl.CostEstimate(
        flops=int(micros * 1.1e9), bytes_accessed=int(micros * 3.0e6), transcendentals=0
    )


def flip(value, axis, bit):
    size = lax.axis_size(axis)
    return lax.ppermute(value, axis, [(i, i ^ bit) for i in range(size)])


def after(value, *marks):
    return lax.optimization_barrier((value,) + marks)[0]


def dot_nn(left, right):
    return lax.dot_general(left, right, (((1,), (0,)), ((), ())), preferred_element_type=F32)


def dot_nt(left, right):
    return lax.dot_general(left, right, (((1,), (1,)), ((), ())), preferred_element_type=F32)


def dot_tn(left, right):
    return lax.dot_general(left, right, (((0,), (0,)), ((), ())), preferred_element_type=F32)


def attend_kernel(
    q_ref, k_ref, v_ref, lmix_ref, wmix_ref, qseg_ref, qpos_ref, kseg_ref, kpos_ref,
    prob_ref, head_ref, out_ref, acc_ref,
):
    step = pl.program_id(0)

    @pl.when(step == 0)
    def _():
        acc_ref[...] = jnp.zeros_like(acc_ref)

    queries = q_ref[...].astype(F32)
    keys = k_ref[...]
    values = v_ref[...]
    visible = (qseg_ref[...] == kseg_ref[...]) & (kpos_ref[...] <= qpos_ref[...])
    total = acc_ref[...]

    def product(i):
        scaled = queries * lmix_ref[i]
        high = scaled.astype(BF16)
        rest = (scaled - high.astype(F32)).astype(BF16)
        return dot_nt(high, keys) + dot_nt(rest, keys)

    ahead = product(0)
    for i in range(HEAD_BLOCK):
        mixed = jnp.where(visible, ahead, -jnp.inf)
        if i + 1 < HEAD_BLOCK:
            ahead = product(i + 1)
        top = jnp.max(mixed, -1, keepdims=True)
        raised = jnp.exp(mixed - top)
        probs = (raised * (1.0 / jnp.sum(raised, -1, keepdims=True))).astype(BF16)
        prob_ref[i] = probs
        heads = dot_nn(probs, values)
        head_ref[i] = heads.astype(BF16)
        total = total + heads * wmix_ref[i]
    acc_ref[...] = total

    @pl.when(step == pl.num_programs(0) - 1)
    def _():
        out_ref[...] = total.astype(BF16)


def attend(queries, keys, values, lmix, wmix, qseg, qpos, kseg, kpos):
    rows, width = queries.shape
    cols = keys.shape[0]
    heads = lmix.shape[0]

    def whole(shape):
        return pl.BlockSpec(shape, lambda i: (0,) * len(shape))

    def per_head(*shape):
        return pl.BlockSpec((HEAD_BLOCK,) + shape, lambda i: (i, 0, 0))

    return pl.pallas_call(
        attend_kernel,
        grid=(heads // HEAD_BLOCK,),
        in_specs=[
            whole((rows, width)),
            whole((cols, width)),
            whole((cols, width)),
            per_head(1, width),
            per_head(1, width),
            whole((rows, 1)),
            whole((rows, 1)),
            whole((1, cols)),
            whole((1, cols)),
        ],
        out_specs=[per_head(rows, cols), per_head(rows, width), whole((rows, width))],
        out_shape=[
            jax.ShapeDtypeStruct((heads, rows, cols), BF16),
            jax.ShapeDtypeStruct((heads, rows, width), BF16),
            jax.ShapeDtypeStruct((rows, width), BF16),
        ],
        scratch_shapes=[pltpu.VMEM((rows, width), F32)],
        compiler_params=pltpu.CompilerParams(vmem_limit_bytes=VMEM_LIMIT),
        cost_estimate=cost(12),
        name="attend",
    )(queries, keys, values, lmix, wmix, qseg, qpos, kseg, kpos)


def back_values_kernel(prob_ref, dao_ref, wmix_ref, dy_ref, out_ref, acc_ref):
    step = pl.program_id(0)

    @pl.when(step == 0)
    def _():
        acc_ref[...] = jnp.zeros_like(acc_ref)

    outer = dao_ref[...].astype(F32)
    scaled = [(outer * wmix_ref[i]).astype(BF16) for i in range(HEAD_BLOCK)]
    all_probs = prob_ref[...].reshape(-1, prob_ref.shape[2])
    acc_ref[...] += dot_tn(all_probs, jnp.concatenate(scaled, 0))

    @pl.when(step == pl.num_programs(0) - 1)
    def _():
        write_halves(out_ref, acc_ref[...].astype(BF16), dy_ref[...])


def write_halves(out_ref, upper, lower):
    rows = upper.shape[0]
    half = out_ref.shape[2]
    for i in range(2):
        out_ref[i, :rows] = upper[:, i * half : (i + 1) * half]
        out_ref[i, rows:] = lower[:, i * half : (i + 1) * half]


def back_values(probs, outer, wmix, grad_rows):
    heads, rows, cols = probs.shape
    width = outer.shape[1]

    def whole(shape):
        return pl.BlockSpec(shape, lambda i: (0,) * len(shape))

    def per_head(*shape):
        return pl.BlockSpec((HEAD_BLOCK,) + shape, lambda i: (i, 0, 0))

    return pl.pallas_call(
        back_values_kernel,
        grid=(heads // HEAD_BLOCK,),
        in_specs=[
            per_head(rows, cols), whole((rows, width)), per_head(1, width), whole((rows, width)),
        ],
        out_specs=whole((2, cols + rows, width // 2)),
        out_shape=jax.ShapeDtypeStruct((2, cols + rows, width // 2), BF16),
        scratch_shapes=[pltpu.VMEM((cols, width), F32)],
        compiler_params=pltpu.CompilerParams(vmem_limit_bytes=VMEM_LIMIT),
        cost_estimate=cost(4),
        name="back_values",
    )(probs, outer, wmix, grad_rows)


def attend_back_kernel(
    prob_ref, head_ref, q_ref, k_ref, v_ref, dao_ref, lmix_ref, wmix_ref,
    out_ref, lsum_ref, wsum_ref, dq_acc, dk_acc,
):
    step = pl.program_id(0)

    @pl.when(step == 0)
    def _():
        dq_acc[...] = jnp.zeros_like(dq_acc)
        dk_acc[...] = jnp.zeros_like(dk_acc)

    queries = q_ref[...].astype(F32)
    outer = dao_ref[...].astype(F32)
    keys = k_ref[...]
    values = v_ref[...]
    dq_sum = dq_acc[...]
    scaled_q = [(queries * lmix_ref[i]).astype(BF16) for i in range(HEAD_BLOCK)]
    scaled_out = [(outer * wmix_ref[i]).astype(BF16) for i in range(HEAD_BLOCK)]
    grads = []
    ahead = dot_nt(scaled_out[0], values)
    for i in range(HEAD_BLOCK):
        grad_probs = ahead
        if i + 1 < HEAD_BLOCK:
            ahead = dot_nt(scaled_out[i + 1], values)
        probs = prob_ref[i].astype(F32)
        product = probs * grad_probs
        shift = jnp.sum(product, -1, keepdims=True)
        grad_mixed = (product - probs * shift).astype(BF16)
        grads.append(grad_mixed)
        back = dot_nn(grad_mixed, keys)
        dq_sum = dq_sum + back * lmix_ref[i]
        lsum_ref[i] = jnp.sum(back * queries, 0, keepdims=True)
        wsum_ref[i] = jnp.sum(head_ref[i].astype(F32) * outer, 0, keepdims=True)
    dq_acc[...] = dq_sum
    dk_acc[...] += dot_tn(jnp.concatenate(grads, 0), jnp.concatenate(scaled_q, 0))

    @pl.when(step == pl.num_programs(0) - 1)
    def _():
        write_halves(out_ref, dk_acc[...].astype(BF16), dq_sum.astype(BF16))


def attend_back(probs, heads_out, queries, keys, values, outer, lmix, wmix):
    rows, width = queries.shape
    cols = keys.shape[0]
    heads = lmix.shape[0]
    half = width // 2

    def whole(shape):
        return pl.BlockSpec(shape, lambda i: (0,) * len(shape))

    def per_head(*shape):
        return pl.BlockSpec((HEAD_BLOCK,) + shape, lambda i: (i, 0, 0))

    return pl.pallas_call(
        attend_back_kernel,
        grid=(heads // HEAD_BLOCK,),
        in_specs=[
            per_head(rows, cols),
            per_head(rows, width),
            whole((rows, width)),
            whole((cols, width)),
            whole((cols, width)),
            whole((rows, width)),
            per_head(1, width),
            per_head(1, width),
        ],
        out_specs=[whole((2, cols + rows, half)), per_head(1, width), per_head(1, width)],
        out_shape=[
            jax.ShapeDtypeStruct((2, cols + rows, half), BF16),
            jax.ShapeDtypeStruct((heads, 1, width), F32),
            jax.ShapeDtypeStruct((heads, 1, width), F32),
        ],
        scratch_shapes=[pltpu.VMEM((rows, width), F32), pltpu.VMEM((cols, width), F32)],
        compiler_params=pltpu.CompilerParams(vmem_limit_bytes=VMEM_LIMIT),
        cost_estimate=cost(11),
        name="attend_back",
    )(probs, heads_out, queries, keys, values, outer, lmix, wmix)


def group_rows(lengths, owners, group_id, pieces, tok_dev):
    shards = pieces.shape[0]
    owned = owners == group_id
    quarter = jnp.where(owned, lengths // shards, 0)
    entry_ids = jnp.arange(lengths.shape[0], dtype=jnp.int32)
    earlier = entry_ids[None, :] < entry_ids[:, None]
    offset = jnp.sum(jnp.where(earlier, quarter[None, :], 0), axis=1)
    row_ids = jnp.arange(tok_dev, dtype=jnp.int32)
    inside = (
        owned[None, :]
        & (offset[None, :] <= row_ids[:, None])
        & (row_ids[:, None] < offset[None, :] + quarter[None, :])
    )
    segment = jnp.sum(jnp.where(inside, entry_ids[None, :], 0), axis=1)
    span_rows = jnp.sum(jnp.where(inside, quarter[None, :], 0), axis=1)
    first_rows = jnp.sum(jnp.where(inside, offset[None, :], 0), axis=1)
    position = pieces[:, None] * span_rows[None, :] + row_ids[None, :] - first_rows[None, :]
    return (jnp.tile(segment, shards), position.reshape(-1))


def rms_parts(values):
    inv_scale = lax.rsqrt(jnp.mean(values * values, -1, keepdims=True) + EPS)
    return (values * inv_scale, inv_scale)


def rms_back(grad_out, normed, inv_scale, gain):
    grad_normed = grad_out * gain
    grad_in = inv_scale * (grad_normed - normed * jnp.mean(grad_normed * normed, -1, keepdims=True))
    return grad_in


def gelu_tanh(values):
    return jax.nn.gelu(values, approximate=True)


def gather_rows(own, far):
    near = flip(jnp.concatenate([own, far], 0), "tp", 1)
    n = own.shape[0]
    return jnp.concatenate([own, near[:n], far, near[n:]], 0)


def scatter_near(partial):
    n = partial.shape[-2] // 4
    low = partial.astype(BF16)
    return flip(
        jnp.concatenate([low[..., n : 2 * n, :], low[..., 3 * n :, :]], -2), "tp", 1
    )


def scatter_far(partial, got):
    n = partial.shape[-2] // 4
    first = partial[..., 2 * n : 3 * n, :].astype(F32) + got[..., n:, :].astype(F32)
    first = first.astype(BF16)
    return first, flip(first, "tp", 2)


def scatter_sum(partial, got, back):
    n = partial.shape[-2] // 4
    own = partial[..., :n, :].astype(F32)
    return own + got[..., :n, :].astype(F32) + back.astype(F32)


def fold_near(halves, source):
    return lax.ppermute(halves, "tp", [(source, 1 - source), (2 + source, 3 - source)])


def to_chip(value, core):
    return lax.ppermute(value, "tp", [(core, 2 + core), (2 + core, core)])


def fold_kernel(far_ref, own_send, got_send, own_keep, got_keep, send_ref, keep_ref):
    rows = own_send.shape[1]
    n = rows // 5
    for own, got, out in ((own_send, got_send, send_ref), (own_keep, got_keep, keep_ref)):
        for r in range(4):
            theirs = got[0, (r ^ 1) * n : (r ^ 1) * n + n].astype(F32)
            total = own[0, r * n : r * n + n].astype(F32) + theirs
            out[r * n : r * n + n] = total.astype(out.dtype)
        out[4 * n : rows] = own[0, 4 * n :].astype(out.dtype)
        out[rows:] = got[0, 4 * n :].astype(out.dtype)


def fold(halves, got, far):
    _, rows, half = halves.shape
    total = rows + rows // 5

    def part(other):
        return pl.BlockSpec(
            (1, rows, half), lambda i, far: ((1 - far[0]) if other else far[0], 0, 0)
        )

    return pl.pallas_call(
        fold_kernel,
        grid_spec=pltpu.PrefetchScalarGridSpec(
            num_scalar_prefetch=1,
            grid=(1,),
            in_specs=[part(True), part(True), part(False), part(False)],
            out_specs=[pl.BlockSpec((total, half), lambda i, far: (0, 0))] * 2,
        ),
        out_shape=[
            jax.ShapeDtypeStruct((total, half), BF16), jax.ShapeDtypeStruct((total, half), F32),
        ],
        compiler_params=pltpu.CompilerParams(vmem_limit_bytes=VMEM_LIMIT),
        cost_estimate=cost(2),
        name="fold",
    )(far[None].astype(jnp.int32), halves, got, halves, got)


def grads_kernel(
    me_ref, k_keep, k_far, v_keep, v_far, left_ref, ao_ref, send_ref, keep_ref, cols_ref, low_ref,
):
    core = me_ref[0]
    n = left_ref.shape[0] // 4
    half = cols_ref.shape[1]

    def columns(keep, far):
        for r in range(4):
            theirs = far[(r ^ 2) * n : (r ^ 2) * n + n].astype(F32)
            cols_ref[r * n : r * n + n] = (keep[r * n : r * n + n] + theirs).astype(BF16)
        low_ref[: 2 * n] = keep[4 * n :].astype(BF16)
        low_ref[2 * n :] = far[4 * n :]

    def product(out, which, low_left):
        at = pl.ds(pl.multiple_of(which * half, 128), half)
        out[:, :half] = dot_tn(left_ref[:, at], cols_ref[...]).astype(BF16)
        out[:, half:] = dot_tn(low_left[:, at], low_ref[...]).astype(BF16)

    for which, keep, far, low_left in ((0, k_keep, k_far, left_ref), (1, v_keep, v_far, ao_ref)):

        @pl.when(core == which)
        def _():
            columns(keep, far)
            product(send_ref, 1 - me_ref[1], low_left)
            product(keep_ref, me_ref[1], low_left)


def weight_grads(core, k_keep, k_far, v_keep, v_far, normed_in, attn_rows):
    rows, width = normed_in.shape
    half = width // 2
    me = jnp.stack([core, lax.axis_index("seq") % 2]).astype(jnp.int32)
    return pl.pallas_call(
        grads_kernel,
        grid_spec=pltpu.PrefetchScalarGridSpec(
            num_scalar_prefetch=1,
            grid=(1,),
            in_specs=[
                pl.BlockSpec(v.shape, lambda i, me: (0, 0))
                for v in (k_keep, k_far, v_keep, v_far, normed_in, attn_rows)
            ],
            out_specs=[
                pl.BlockSpec((half, width), lambda i, me: (0, 0)),
                pl.BlockSpec((half, width), lambda i, me: (0, 0)),
                pl.BlockSpec((rows, half), lambda i, me: (0, 0)),
            ],
            scratch_shapes=[pltpu.VMEM((rows, half), BF16)],
        ),
        out_shape=[
            jax.ShapeDtypeStruct((half, width), BF16),
            jax.ShapeDtypeStruct((half, width), BF16),
            jax.ShapeDtypeStruct((rows, half), BF16),
        ],
        compiler_params=pltpu.CompilerParams(vmem_limit_bytes=VMEM_LIMIT),
        cost_estimate=cost(5),
        name="weight_grads",
    )(me, k_keep, k_far, v_keep, v_far, normed_in, attn_rows)


def halves_of(value, bit):
    me = (lax.axis_index("seq") // bit) % 2
    pair = value.reshape((2, -1) + value.shape[1:])
    send = lax.dynamic_index_in_dim(pair, 1 - me, 0, keepdims=False)
    return send, lax.dynamic_index_in_dim(pair, me, 0, keepdims=False)


def seq_levels():
    size = lax.axis_size("seq")
    levels = []
    bit = 2
    while bit < size:
        levels.append((bit, 2 * bit) if 2 * bit < size else (bit,))
        bit *= 4
    return levels


def offsets(bits):
    return [sum(b for i, b in enumerate(bits) if (n >> i) & 1) for n in range(1, 1 << len(bits))]


def line_swap(value):
    size = lax.axis_size("seq")
    groups = [list(range(low, size, 2)) for low in range(2)]
    return lax.all_to_all(value, "seq", 0, 0, axis_index_groups=groups, tiled=True)


def line_sum(value, *marks):
    me = lax.axis_index("seq")
    for bits in seq_levels()[::-1]:
        count = 1 << len(bits)
        blocks = value.reshape((count, -1) + value.shape[1:])

        def pick(which):
            at = sum(((which // b) % 2) << i for i, b in enumerate(bits))
            return lax.dynamic_index_in_dim(blocks, at, 0, keepdims=False)

        got = [flip(pick(me ^ off), "seq", off) for off in offsets(bits)]
        total = after(pick(me), *marks).astype(F32)
        for piece in got:
            total = total + piece.astype(F32)
        value = total.astype(BF16)
    return value


def line_gather(block):
    value, ids = block[None], [0]
    for bits in seq_levels():
        got = [flip(value, "seq", off) for off in offsets(bits)]
        ids = ids + [i ^ off for off in offsets(bits) for i in ids]
        value = jnp.concatenate([value] + got, 0)
    return value, [i // 2 for i in ids]


def all_sum(value):
    for axis in ("seq", "tp"):
        bit = 1
        while bit < lax.axis_size(axis):
            value = value + flip(value, axis, bit)
            bit *= 2
    return value


def tp_sum(value):
    for bit in (1, 2):
        value = value + flip(value, "tp", bit)
    return value


def row_vector(column):
    wide = jnp.broadcast_to(column, (column.shape[0], 128))
    return jnp.transpose(wide)[:1]


def line_rows(value, ids):
    if value.shape[1] % 16 == 0:
        return value, ids
    me = lax.axis_index("seq") // 2
    at = [ids.index(i) for i in range(len(ids))]
    order = jnp.take(jnp.array(at, jnp.int32), jnp.arange(len(ids), dtype=jnp.int32) ^ me)
    rows = jnp.take(value, order, axis=0).reshape(1, -1, value.shape[2])
    return rows.reshape((2, -1) + rows.shape[2:]), None


def spread(value, ids, *marks):
    half = value.shape[0] // 2
    over_y = flip(value, "seq", 1)
    over_x = flip(value, "tp", 2)
    over_y = after(over_y, *marks)
    sent = (over_y[:half], over_x[half:])
    corner_low = flip(sent[0], "tp", 2)
    corner_high = flip(sent[1], "seq", 1)
    low, high = (ids[:half], ids[half:]) if ids else (None, None)
    return [
        (value, ids, 0, 0, 0, 0),
        (over_y, ids, 1, 0, 0, 0),
        (over_x, ids, 0, 1, 0, 0),
        (corner_low, low, 1, 1, 0, 0),
        (corner_high, high, 1, 1, 0, half),
    ], sent


def spread_core(pieces, *marks):
    held = [after(v, *marks) if at > 2 else v for at, (v, *_) in enumerate(pieces)]
    own = [(h,) + p[1:] for h, p in zip(held, pieces)]
    return own + [(flip(v, "tp", 1), i, y, x, 1, b) for v, i, y, x, _, b in own]


def update_kernel(layout, me_ref, *refs):
    sources, (w_ref, wout_ref), outs = refs[:-11], refs[-11:-9], refs[-9:]
    me_seq, me_far, me_core = me_ref[0], me_ref[1] // 2, me_ref[1] % 2

    def update(core, part, weight, grad, new, rows, cols):
        height, width = grad.shape[1:]
        half = width // 2
        for near in range(2):

            @pl.when((me_core ^ near) == core)
            def _():
                for ref, (ids, y, x, c, first) in zip(sources, layout):
                    if c != near:
                        continue
                    col = pl.multiple_of((me_far ^ x) * half, 128)
                    top = ((me_seq % 2) ^ y) * (height // 2)
                    n = ref.shape[1]
                    for k in range(ref.shape[0]):
                        line = first + k if ids is None else (me_seq // 2) ^ ids[k]
                        at = pl.multiple_of(top + line * n, 16)
                        block = ref[k, :, part * half : (part + 1) * half]
                        grad[0, pl.ds(at, n), pl.ds(col, half)] = block.astype(F32)

        gradient = grad[0]
        squares = gradient * gradient + TINY
        row_means = jnp.sum(squares, -1, keepdims=True) * (1.0 / width)
        col_means = jnp.sum(squares, 0, keepdims=True) * (1.0 / height)
        scale = jnp.sum(row_means, 0, keepdims=True) * (1.0 / height)
        rows[0] = row_vector(row_means)
        cols[0] = col_means
        pace = lax.rsqrt(row_means / scale) * STEP
        new[0] = weight - gradient * pace * lax.rsqrt(col_means)
        return gradient

    for at, (core, part) in enumerate(((0, 1), (0, 0), (1, 0), (1, 1))):

        @pl.when(pl.program_id(0) == at)
        def _():
            if at == 3:
                update(core, part, wout_ref[0], *outs[4:8])
                return
            weight = w_ref[0]
            gradient = update(core, part, weight, *outs[:4])
            dots = weight.astype(BF16).astype(F32) * gradient
            dots = row_vector(jnp.sum(dots, -1, keepdims=True))
            outs[8][...] = dots if at == 0 else outs[8][...] + dots


def attn_update(pieces, w_qkv, w_out):
    width = w_qkv.shape[1]
    me = jnp.stack([lax.axis_index("seq"), lax.axis_index("tp")]).astype(jnp.int32)

    def whole(shape):
        return pl.BlockSpec(shape, lambda i, me: (0,) * len(shape))

    def by_step(shape):
        return pl.BlockSpec((1,) + shape, lambda i, me: (jnp.minimum(i, 2), 0, 0))

    shapes = [(width, width), (width, width), (1, width), (1, width)]
    return pl.pallas_call(
        functools.partial(update_kernel, [p[1:] for p in pieces]),
        grid_spec=pltpu.PrefetchScalarGridSpec(
            num_scalar_prefetch=1,
            grid=(4,),
            in_specs=[whole(p[0].shape) for p in pieces]
            + [by_step((width, width)), whole((1, width, width))],
            out_specs=[by_step(shape) for shape in shapes]
            + [whole((1,) + shape) for shape in shapes]
            + [whole((1, width))],
        ),
        out_shape=[jax.ShapeDtypeStruct((3,) + shape, F32) for shape in shapes]
        + [jax.ShapeDtypeStruct((1,) + shape, F32) for shape in shapes]
        + [jax.ShapeDtypeStruct((1, width), F32)],
        compiler_params=pltpu.CompilerParams(vmem_limit_bytes=VMEM_LIMIT),
        cost_estimate=cost(14),
        name="attn_update",
    )(me, *[p[0] for p in pieces], w_qkv, w_out[None])


def collect_kernel(step, me_ref, own_ref, over_ref, grad_ref, rows_ref, cols_ref):
    lines, _, n, width = own_ref.shape
    for off, ref in enumerate((own_ref, over_ref)):
        for line in range(lines):
            at = pl.multiple_of((me_ref[0] ^ off) * (lines * n if step == 1 else n), 16)
            at = at + line * step * n
            grad_ref[pl.ds(at, n)] = ref[line, 0].astype(F32)
    gradient = grad_ref[...]
    squares = gradient * gradient + TINY
    rows_ref[...] = row_vector(jnp.sum(squares, -1, keepdims=True))
    cols_ref[...] = jnp.sum(squares, 0, keepdims=True)


def collect(own, over, which, step, micros):
    me = lax.axis_index("seq") % 2
    if own.shape[2] % 16:
        pair = jnp.where(me == 0, jnp.stack([own, over]), jnp.stack([over, own]))[:, :, which]
        pair = pair if step == 1 else pair.swapaxes(0, 1)
        full = pair.reshape(2, 1, -1, own.shape[3])
        own, over, which, step, me = full[:1], full[1:], 0, 1, jnp.int32(0)
    lines, _, n, width = own.shape
    height = 2 * lines * n
    source = pl.BlockSpec((lines, 1, n, width), lambda i, me: (0, which, 0, 0))
    shapes = [(height, width), (1, height), (1, width)]
    grad, rows, cols = pl.pallas_call(
        functools.partial(collect_kernel, step),
        grid_spec=pltpu.PrefetchScalarGridSpec(
            num_scalar_prefetch=1,
            grid=(1,),
            in_specs=[source, source],
            out_specs=[pl.BlockSpec(shape, lambda i, me: (0, 0)) for shape in shapes],
        ),
        out_shape=[jax.ShapeDtypeStruct(shape, F32) for shape in shapes],
        compiler_params=pltpu.CompilerParams(vmem_limit_bytes=VMEM_LIMIT),
        cost_estimate=cost(micros),
        name="collect",
    )(me[None].astype(jnp.int32), own, over)
    return grad, rows[0], cols[0]


def per_device(
    layer_input,
    cotangent,
    seq_lengths,
    seq_group,
    norm1_gain,
    w_qkv,
    mix_logits,
    mix_weights,
    w_attn_out,
    norm2_gain,
    w_up,
    w_down,
):
    shards = lax.axis_size("tp")
    groups = lax.axis_size("seq")
    shard_id = lax.axis_index("tp")
    group_id = lax.axis_index("seq")
    tok_dev = layer_input.shape[1]
    width = layer_input.shape[2]
    half = width // 2
    head_count = mix_logits.shape[0]
    head_dim = width // head_count
    core = shard_id % 2
    far = shard_id // 2
    group_n = tok_dev * shards
    lines = groups // 2

    own_x = layer_input[0]
    far_x = flip(own_x, "tp", 2)
    pieces = shard_id ^ jnp.arange(shards, dtype=jnp.int32)
    segment, position = group_rows(seq_lengths, seq_group, group_id, pieces, tok_dev)
    lmix = jnp.repeat(mix_logits.T * head_dim**-0.5, head_dim, axis=1)[:, None, :]
    wmix = jnp.repeat(mix_weights, head_dim, axis=1)[:, None, :]
    qkv_b = w_qkv.astype(BF16)
    far_x = after(far_x, qkv_b, lmix, wmix, segment, position)
    inputs_b = gather_rows(own_x, far_x)
    own_cot = after(cotangent[0], far_x)
    far_cot = flip(own_cot, "tp", 2)

    inputs = inputs_b.astype(F32)
    normed1, inv1 = rms_parts(inputs)
    normed_in = (normed1 * norm1_gain).astype(BF16)
    normed1_own = normed1[:tok_dev]
    inv1_own = inv1[:tok_dev]
    queries = jnp.dot(normed_in[:tok_dev], qkv_b[0], preferred_element_type=F32).astype(BF16)
    keys = jnp.dot(normed_in, qkv_b[1], preferred_element_type=F32).astype(BF16)
    values = jnp.dot(normed_in, qkv_b[2], preferred_element_type=F32).astype(BF16)

    probs, heads_out, attn_own = attend(
        queries,
        keys,
        values,
        lmix,
        wmix,
        segment[:tok_dev, None],
        position[:tok_dev, None],
        segment[None, :],
        position[None, :],
    )
    far_ao = flip(attn_own, "tp", 2)
    cot_b = gather_rows(own_cot, after(far_cot, attn_own))
    out_b = after(w_attn_out, attn_own).astype(BF16)
    up_b = after(w_up, attn_own).astype(BF16)
    down_b = after(w_down, attn_own).astype(BF16)
    grad_act = jnp.einsum("nd,fd->nf", cot_b, down_b, preferred_element_type=F32)
    far_ao = after(far_ao, grad_act, out_b, up_b)
    attn_rows = gather_rows(attn_own, far_ao)

    residual = inputs + jnp.dot(attn_rows, out_b, preferred_element_type=F32)
    normed2, inv2 = rms_parts(residual)
    normed_mid = (normed2 * norm2_gain).astype(BF16)
    up_pre = jnp.dot(normed_mid, up_b, preferred_element_type=F32)
    activated, gelu_back = jax.vjp(gelu_tanh, up_pre)
    act_b = activated.astype(BF16)
    grad_up_in = gelu_back(grad_act)[0].astype(BF16)
    mid_part = jnp.einsum("nf,df->nd", grad_up_in, up_b, preferred_element_type=F32)
    mid_got = scatter_near(mid_part)
    act_b, ignored = lax.optimization_barrier((act_b, mid_part))
    grad_down = dot_tn(act_b, cot_b).astype(BF16)
    mid_got = after(mid_got, grad_down)
    mid_first, mid_back = scatter_far(mid_part, mid_got)
    grad_up = dot_tn(after(normed_mid, mid_first), grad_up_in).astype(BF16)
    down_send, down_keep = halves_of(after(grad_down, mid_first), 1)
    down_got = flip(down_send, "seq", 1)
    up_lines = line_swap(grad_up.reshape(lines, -1, width))
    mid_back = after(mid_back, grad_up)
    grad_mid = scatter_sum(mid_part, mid_got, mid_back)

    grad_res_norm = rms_back(grad_mid, normed2[:tok_dev], inv2[:tok_dev], norm2_gain)
    grad_res = own_cot.astype(F32) + grad_res_norm
    grad_res_b = grad_res.astype(BF16)
    grad_heads = dot_nt(grad_res_b, out_b).astype(BF16)
    v_halves = back_values(probs, grad_heads, wmix, grad_res_b)
    v_got = fold_near(v_halves, 0)
    down_half = (after(down_keep, v_halves).astype(F32) + down_got.astype(F32)).astype(BF16)
    k_halves, lsum, wsum = attend_back(
        probs, heads_out, queries, keys, values, after(grad_heads, v_halves, down_half), lmix, wmix
    )
    k_got = fold_near(k_halves, 1)

    v_send, v_keep = fold(v_halves, after(v_got, k_halves), far)
    v_far = to_chip(v_send, 1)
    up_sum = jnp.sum(after(up_lines, v_send).astype(F32), 0).astype(BF16)
    up_send, up_keep = halves_of(up_sum, 1)
    up_got = flip(up_send, "seq", 1)
    down_lines = line_swap(after(down_half, up_sum).reshape(lines, -1, width))
    k_send, k_keep = fold(k_halves, after(k_got, up_sum), far)
    k_far = to_chip(k_send, 0)
    branch = jnp.dot(after(act_b, k_send), down_b, preferred_element_type=F32).astype(BF16)
    down_block = jnp.sum(after(down_lines, k_send).astype(F32), 0)
    up_block = after(up_keep, k_send).astype(F32) + up_got.astype(F32)
    ffn_block = jnp.stack([down_block, up_block]).astype(BF16)
    ffn_spread = jnp.broadcast_to(ffn_block[None], (lines,) + ffn_block.shape)
    ffn_line = line_swap(ffn_spread)
    send, keep, first_cols = weight_grads(
        core, k_keep, after(k_far, ffn_spread, branch), v_keep, v_far, normed_in, attn_rows
    )
    got = flip(send, "seq", 1)

    first_w = lax.dynamic_slice(
        lax.dynamic_index_in_dim(qkv_b, 1 + core, 0, keepdims=False), (0, far * half), (width, half)
    )
    in_part = dot_nt(after(first_cols, keep), first_w)
    rows_part = jnp.stack([in_part.astype(BF16), branch])
    rows_got = scatter_near(rows_part)
    dq_own = jnp.concatenate([k_halves[0, group_n:], k_halves[1, group_n:]], 1)
    dh_own = dot_nt(after(dq_own, keep), qkv_b[0])
    rows_first, rows_back = scatter_far(rows_part, rows_got)
    grad_mix_logits = (
        jnp.sum(lsum.reshape(head_count, head_count, head_dim), -1).T * head_dim**-0.5
    )
    grad_mix_weights = jnp.sum(wsum.reshape(head_count, head_count, head_dim), -1)
    mixes = jnp.stack([grad_mix_logits, grad_mix_weights]).reshape(-1)

    mixes = after(mixes, keep)
    for axis, bit in (("tp", 2), ("tp", 1)):
        mixes = mixes + flip(mixes, axis, bit)
    half_sum = (after(keep, mixes).astype(F32) + got.astype(F32)).astype(BF16)
    mixes = after(mixes, half_sum)
    mixes = mixes + flip(mixes, "seq", 1)
    block = line_sum(half_sum, rows_first, ffn_line, mixes)
    ffn_over = flip(after(ffn_line, half_sum), "seq", 1)
    rows_sum = scatter_sum(rows_part, rows_got, after(rows_back, block))
    block_out = (rows_sum[1] + residual[:tok_dev]).astype(BF16)[None]
    grad_in_norm = rms_back(rows_sum[0] + dh_own, normed1_own, inv1_own, norm1_gain)
    input_grad = grad_res + grad_in_norm
    line, line_ids = line_rows(*line_gather(block))
    line = after(line, block_out)
    grad_down, down_rowsum, down_colsum = collect(ffn_line, after(ffn_over, block), 0, 1, 10)
    line = after(line, grad_down)
    grad_up, up_rowsum, up_colsum = collect(ffn_line, after(ffn_over, line), 1, 2, 2)
    grad_norm2 = jnp.sum(up_b.astype(F32) * grad_up, 1) / norm2_gain
    mixes = after(mixes, line)
    for bit in [2 << i for i in range(10) if 2 << i < groups]:
        mixes = mixes + flip(mixes, "seq", bit)
    shard_pieces, sent = spread(line, line_ids, grad_up, mixes)
    full_hidden = w_up.shape[1] * shards
    totals = after(tp_sum(jnp.stack([up_rowsum, down_colsum, grad_norm2])), *sent)
    up_rows = totals[0] / full_hidden
    down_cols = totals[1] / full_hidden
    grad_norm2 = totals[2]
    up_cols = up_colsum / width
    down_rows = down_rowsum / width
    up_pace = lax.rsqrt(up_rows / jnp.mean(up_rows)) * STEP
    new_up = w_up - grad_up * up_pace[:, None] * lax.rsqrt(up_cols)[None, :]
    down_pace = lax.rsqrt(down_cols / jnp.mean(down_cols)) * STEP
    new_down = w_down - grad_down * lax.rsqrt(down_rows)[:, None] * down_pace[None, :]
    shard_pieces = spread_core(shard_pieces, new_up, new_down)
    mixes = mixes.reshape(2, head_count, head_count)
    updated = attn_update(shard_pieces, w_qkv, w_attn_out)
    grad_qkv, new_qkv, qkv_rows, qkv_cols, grad_o, new_o, out_rows, out_cols, dots = updated
    grad_norm1 = dots[0] / norm1_gain
    grad_mix_logits = mixes[0]
    grad_mix_weights = mixes[1]
    return (
        block_out,
        input_grad[None],
        grad_norm1,
        grad_qkv,
        grad_mix_logits,
        grad_mix_weights,
        grad_o[0],
        grad_norm2,
        grad_up,
        grad_down,
        qkv_rows[:, 0],
        qkv_cols[:, 0],
        out_rows[0, 0],
        out_cols[0, 0],
        up_rows,
        up_cols,
        down_rows,
        down_cols,
        new_qkv,
        new_o[0],
        new_up,
        new_down,
    )


def solution(mesh):
    return jax.shard_map(
        per_device,
        mesh=mesh,
        in_specs=(
            P("seq", "tp", None),
            P("seq", "tp", None),
            P(),
            P(),
            P(),
            P(),
            P(),
            P(),
            P(),
            P(),
            P(None, "tp"),
            P("tp", None),
        ),
        out_specs=(
            P("seq", "tp", None),
            P("seq", "tp", None),
            P(),
            P(),
            P(),
            P(),
            P(),
            P(),
            P(None, "tp"),
            P("tp", None),
            P(),
            P(),
            P(),
            P(),
            P(),
            P("tp"),
            P("tp"),
            P(),
            P(),
            P(),
            P(None, "tp"),
            P("tp", None),
        ),
        check_vma=False,
    )
```

time: 712 us -> 249 us (0.35)
  matrix products: 381 us -> 22.1 us
  blocking collectives: 69.8 us -> 0 us
  other arithmetic: 107 us -> 46.9 us
  Pallas kernels: 0 us -> 58.3 us
  starting transfers between devices: 0.16 us -> 51.7 us
  waiting for transfers between devices: 86.8 us -> 48.1 us
  local copies, waits for them, and re-layouts: 44 us -> 14.6 us
  between operations: 16.7 us -> 3.15 us
    dot_general x24 -> x13, matrix products: 381 us -> 22.1 us  [the longest x3 5.23 us: dot_nt(): lax.dot_general(left, right, (((1,), (1,)), ((), ())), preferred_element_...]
    psum x3 -> x0, waiting for transfers between devices: 86.8 us -> none  [the longest x1 78 us: per_device(): lax.psum((grad_norm1, grad_qkv, logit_mix_sum, weight_mix_sum, grad_attn_...]
    pallas_call x0 -> x9, Pallas kernels: none -> 58.3 us  [the longest x1 15.9 us: attn_update(): pl.pallas_call(functools.partial(update_kernel, [p[1:] for p in pieces]),...]
    psum x2 -> x0, blocking collectives: 48.6 us -> none  [the longest x1 41.6 us: per_device(): lax.psum((grad_norm1, grad_qkv, logit_mix_sum, weight_mix_sum, grad_attn_...]
    dot_general x2 -> x0, other arithmetic: 48.5 us -> none  [pair_total(): return jnp.einsum('gqk,hqk->gh', first_stack, second_stack, precision=HIGH)]
    ppermute x0 -> x40, waiting for transfers between devices: none -> 43.9 us  [the longest x36 43.9 us: flip(): return lax.ppermute(value, axis, [(i, i ^ bit) for i in range(size)])]
    ppermute x0 -> x40, starting transfers between devices: none -> 38.1 us  [the longest x36 29.6 us: flip(): return lax.ppermute(value, axis, [(i, i ^ bit) for i in range(size)])]
    reduce_sum x11 -> x7, other arithmetic: 32.3 us -> 4.61 us  [the longest x1 2.1 us: per_device(): grad_norm2 = jnp.sum(up_b.astype(F32) * grad_up, 1) / norm2_gain]
  transfers between devices with their start and end apart: 4 -> 43, of which waited for: 2 -> 16; matrix products, arithmetic and copies ran while one was open for 48% -> 26% of each run, Pallas kernels for 0% -> 17%
where the time goes in v1:
time: 249 us; the launch traced here: 245 us
  Pallas kernels  58.3 us (23%)
  starting transfers between devices  51.7 us (21%)
  waiting for transfers between devices  48.1 us (19%)
  other arithmetic  46.9 us (19%)
  matrix products  22.1 us (9%)
  local copies, waits for them, and re-layouts  14.6 us (6%)
  between operations  3.15 us (1%)
    ppermute x36, waiting for transfers between devices, flip(): return lax.ppermute(value, axis, [(i, i ^ bit) for i in range(size)])  43.9 us
    ppermute x36, starting transfers between devices, flip(): return lax.ppermute(value, axis, [(i, i ^ bit) for i in range(size)])  29.6 us
    pallas_call x1, Pallas kernels, attn_update(): pl.pallas_call(functools.partial(update_kernel, [p[1:] for p in pieces]),...  15.9 us
    all_to_all x3, starting transfers between devices, line_swap(): lax.all_to_all(value, 'seq', 0, 0, axis_index_groups=groups, tiled=True)  13.7 us
    pallas_call x1, Pallas kernels, attend(): pl.pallas_call(attend_kernel, grid=(heads // HEAD_BLOCK,), in_specs=[whol...  12.5 us
    pallas_call x1, Pallas kernels, attend_back(): pl.pallas_call(attend_back_kernel, grid=(heads // HEAD_BLOCK,), in_specs=...  12.4 us
    sub x1, other arithmetic, per_device(): w_down - grad_down * lax.rsqrt(down_rows)[:, None] * down_pace[None, :]  6.64 us
    unnamed x94, local copies, waits for them, and re-layouts  6.22 us
  transfers between devices with their start and end apart: 43, of which 16 were waited for; matrix products, arithmetic and copies ran while one was open for 26% of the time, Pallas kernels for 17%

profile of v1, /device:TPU:0, one launch (start us, length us, event | category | flops | bytes accessed | tf_op | source)
XLA Modules:
  0.0 245.0 jit_solution(12135107221700883189)
XLA Ops:
  0.7 3.0 %collective-permute-start = (bf16[160,768]{1,0:T(8,128)(2,1)}, bf16[160,768]{1,0:T(8,128)(2,1)S(1)}, u32[]{:S(2)}, u32[]{:S(2)}) collective-permute-start(bf16[160,768]{1,0:T(8,128)(2,1)} %bitcast.107), channel_id=1, source_target_pairs={{0,2},{1,3},{2,0},{3,1},{4,6},{5,7},{6,4},{7,5},{8,10},{9,11},{10,... | collective-permute-start | bytes 737288 | tf_op jit(solution)/shard_map/ppermute | solution.py:27
  5.1 5.2 %convert_element_type.145 = bf16[3,768,768]{2,1,0:T(8,128)(2,1)} convert(f32[3,768,768]{2,1,0:T(8,128)} %refs_10_.1) | non-fusion elementwise | flops 1769472 | bytes 10616832 | tf_op jit(solution)/shard_map/convert_element_type | solution.py:682
  13.3 1.6 convert_multiply_fusion
  18.3 12.5 %attend.1 = (bf16[12,160,640]{2,1,0:T(8,128)(2,1)S(1)}, bf16[12,160,768]{2,1,0:T(8,128)(2,1)}, bf16[160,768]{1,0:T(8,128)(2,1)S(1)}) custom-call(bf16[160,768]{1,0:T(8,128)(2,1)S(1)} %convolution_convert_fusion.7.q_ref, bf16[640,768]{1,0:T(8,128)(2,1)S(1)} %convolution_convert_fusion.5.k_ref, bf16[640,768]{1,0:T(8,128)(2,1)S(1)} %convolution_convert_fusion.4.v_ref, ...), custom_call_target="tpu_custom_call" | custom-call | flops 13200000000 | bytes 36000000 | tf_op jit(solution)/shard_map/attend/pallas_call | solution.py:98
  30.8 1.3 pad_maximum_fusion.7
  34.1 1.9 copy-done.18
  36.0 1.9 fusion.13
  37.9 2.6 %collective-permute-done.2 = bf16[160,768]{1,0:T(8,128)(2,1)S(1)} collective-permute-done((bf16[160,768]{1,0:T(8,128)(2,1)S(1)}, bf16[160,768]{1,0:T(8,128)(2,1)S(1)}, u32[]{:S(2)}, u32[]{:S(2)}) %collective-permute-start.2) | collective-permute-done | bytes 245792 | tf_op jit(solution)/shard_map/ppermute | solution.py:27
  40.6 1.9 collective-permute-done.5
  43.7 1.8 multiply_convert_fusion.1
  45.5 3.0 %multiply_convert_fusion = (bf16[640,768]{1,0:T(8,128)(2,1)}, bf16[640,768]{1,0:T(8,128)(2,1)S(1)}) fusion(f32[640,768]{1,0:T(8,128)S(1)} %fusion.13, bf16[640,768]{1,0:T(8,128)(2,1)S(1)} %get-tuple-element.101, bf16[768,768]{1,0:T(8,128)(2,1)S(1)} %convert_element_type.154), kind=kOutput, calls=%fused_computation.22 | convolution fusion | flops 765788160 | bytes 6094848 | tf_op jit(solution)/shard_map/dot_general | solution.py:720
  48.5 2.2 fusion.42
  51.8 2.5 %convolution_convert_fusion.1 = bf16[768,768]{1,0:T(8,128)(2,1)S(1)} fusion(bf16[640,768]{1,0:T(8,128)(2,1)} %get-tuple-element.116, bf16[160,768]{1,0:T(8,128)(2,1)} %copy-done.36, bf16[160,768]{1,0:T(8,128)(2,1)S(1)} %copy-done.34, bf16[160,768]{1,0:T(8,128)(2,1)} %copy-done.35, bf16[160,768]{1,0:T(8,128)(2,1)} %bitcast.10), kind=kOutput, calls=%fused_computation.27 | convolution fusion | flops 759496704 | bytes 3145728 | tf_op jit(solution)/shard_map/dot_general | solution.py:43
  54.3 2.0 fusion.19
  58.2 1.5 collective-permute-start.8
  59.7 2.1 convolution_convert_fusion
  61.9 5.2 %all-to-all-start = ((bf16[4,192,768]{2,1,0:T(8,128)(2,1)}), bf16[4,192,768]{2,1,0:T(8,128)(2,1)}, u32[]{:S(2)}, u32[]{:S(2)}) async-start(bf16[4,192,768]{2,1,0:T(8,128)(2,1)} %bitcast.112), calls=%async_computation | async-start | bytes 2359296 | tf_op jit(solution)/shard_map/all_to_all | solution.py:445
  67.1 1.5 multiply_reduce_fusion.3
  68.6 2.5 %fusion.36 = (bf16[160,768]{1,0:T(8,128)(2,1)S(1)}, f32[160,768]{1,0:T(8,128)}) fusion(f32[160]{0:T(256)S(1)} %broadcast_multiply_fusion.2, f32[640,768]{1,0:T(8,128)} %get-tuple-element.169, f32[768]{0:T(1024)S(1)} %copy-done.37, bf16[160,768]{1,0:T(8,128)(2,1)S(1)} %collective-permute-done.7, bf16[320,768]{1,0:T(8,128)(2,1)} %copy-done.23, ...), kind=kLoop, calls=%fused_computation.139 | loop fusion | flops 1351680 | bytes 2461952 | tf_op jit(solution)/shard_map/convert_element_type | solution.py:739
  71.7 3.8 %back_values.1.own_send.own_keep = bf16[2,800,384]{2,1,0:T(8,128)(2,1)} custom-call(bf16[12,160,640]{2,1,0:T(8,128)(2,1)S(1)} %copy-done.7, bf16[160,768]{1,0:T(8,128)(2,1)S(1)} %convolution_convert_fusion.6.dao_ref, f32[12,1,768]{2,1,0:T(1,128)S(1)} %broadcast_in_dim_reshape.8.wmix_ref, bf16[160,768]{1,0:T(8,128)(2,1)S(1)} %get-tuple-element.166.dy_ref), custom_call_target="tpu_custom_call" | custom-call | flops 4400000000 | bytes 12000000 | tf_op jit(solution)/shard_map/back_values/pallas_call | solution.py:160
  75.5 2.5 %collective-permute-start.10 = (bf16[2,800,384]{2,1,0:T(8,128)(2,1)}, bf16[2,800,384]{2,1,0:T(8,128)(2,1)}, u32[]{:S(2)}, u32[]{:S(2)}) collective-permute-start(bf16[2,800,384]{2,1,0:T(8,128)(2,1)} %back_values.1.own_send.own_keep), channel_id=1, source_target_pairs={{0,1},{2,3},{4,5},{6,7},{8,9},{10,11},{12,13},{14,15},{16,17},{18,... | collective-permute-start | bytes 3686408 | tf_op jit(solution)/shard_map/ppermute | solution.py:317
  77.9 2.1 add_convert_fusion.1
  80.0 12.4 %attend_back.1 = (bf16[2,800,384]{2,1,0:T(8,128)(2,1)}, f32[12,1,768]{2,1,0:T(1,128)S(1)}, f32[12,1,768]{2,1,0:T(1,128)S(1)}) custom-call(bf16[12,160,640]{2,1,0:T(8,128)(2,1)} %copy-done.6, bf16[12,160,768]{2,1,0:T(8,128)(2,1)} %get-tuple-element.91.head_ref, bf16[160,768]{1,0:T(8,128)(2,1)S(1)} %convolution_convert_fusion.7.q_ref, ...), custom_call_target="tpu_custom_call" | custom-call | flops 12099999744 | bytes 33000000 | tf_op jit(solution)/shard_map/attend_back/pallas_call | solution.py:228
  92.4 1.3 collective-permute-start.9
  94.8 2.7 %fold.2 = (bf16[960,384]{1,0:T(8,128)(2,1)}, f32[960,384]{1,0:T(8,128)S(1)}) custom-call(s32[1]{0:T(128)} %bitcast.2.far_ref, bf16[2,800,384]{2,1,0:T(8,128)(2,1)} %back_values.1.own_send.own_keep, bf16[2,800,384]{2,1,0:T(8,128)(2,1)} %collective-permute-done.10.got_send.got_keep, bf16[2,800,384]{2,1,0:T(8,128)(2,1)} %back_values.1.own_send.own_keep, ...), custom_call_target="tpu_custom_call" | custom-call | flops 2200000000 | bytes 6000000 | tf_op jit(solution)/shard_map/fold/pallas_call | solution.py:345
  98.6 1.5 collective-permute-start.13
  100.1 1.5 reduce_sum.145
  101.6 5.0 %all-to-all-start.1 = ((bf16[4,96,768]{2,1,0:T(8,128)(2,1)}), bf16[4,96,768]{2,1,0:T(8,128)(2,1)S(1)}, u32[]{:S(2)}, u32[]{:S(2)}) async-start(bf16[4,96,768]{2,1,0:T(8,128)(2,1)} %bitcast.15), calls=%async_computation.1 | async-start | bytes 1179648 | tf_op jit(solution)/shard_map/all_to_all | solution.py:445
  106.6 2.8 %fold.3 = (bf16[960,384]{1,0:T(8,128)(2,1)}, f32[960,384]{1,0:T(8,128)S(1)}) custom-call(s32[1]{0:T(128)} %bitcast.2.far_ref, bf16[2,800,384]{2,1,0:T(8,128)(2,1)} %get-tuple-element.106.own_send.own_keep, bf16[2,800,384]{2,1,0:T(8,128)(2,1)} %collective-permute-done.9.got_send.got_keep, bf16[2,800,384]{2,1,0:T(8,128)(2,1)} %get-tuple-element.106.own_send.own_keep, ...), custom_call_target="tpu_custom_call" | custom-call | flops 2200000000 | bytes 6000000 | tf_op jit(solution)/shard_map/fold/pallas_call | solution.py:345
  109.5 3.2 %collective-permute-start.11 = (bf16[960,384]{1,0:T(8,128)(2,1)}, bf16[960,384]{1,0:T(8,128)(2,1)}, u32[]{:S(2)}, u32[]{:S(2)}) collective-permute-start(bf16[960,384]{1,0:T(8,128)(2,1)} %get-tuple-element.112), channel_id=1, source_target_pairs={{0,2},{2,0},{4,6},{6,4},{8,10},{10,8},{12,14},{14,12},{16,18},{18,... | collective-permute-start | bytes 2211848 | tf_op jit(solution)/shard_map/ppermute | solution.py:321
  113.3 1.9 convolution_convert_fusion.3
  115.2 3.7 %collective-permute-done.12 = bf16[96,768]{1,0:T(8,128)(2,1)S(1)} collective-permute-done((bf16[96,768]{1,0:T(8,128)(2,1)S(1)}, bf16[96,768]{1,0:T(8,128)(2,1)S(1)}, u32[]{:S(2)}, u32[]{:S(2)}) %collective-permute-start.12) | collective-permute-done | bytes 147488 | tf_op jit(solution)/shard_map/ppermute | solution.py:27
  118.9 3.9 %all-to-all-done.1 = bf16[4,96,768]{2,1,0:T(8,128)(2,1)S(1)} async-done(((bf16[4,96,768]{2,1,0:T(8,128)(2,1)}), bf16[4,96,768]{2,1,0:T(8,128)(2,1)S(1)}, u32[]{:S(2)}, u32[]{:S(2)}) %all-to-all-start.1) | async-done | bytes 589856 | tf_op jit(solution)/shard_map/all_to_all | solution.py:445
  124.1 3.5 %all-to-all-start.2 = ((bf16[4,2,96,768]{3,2,1,0:T(8,128)(2,1)}), bf16[4,2,96,768]{3,2,1,0:T(8,128)(2,1)S(1)}, u32[]{:S(2)}, u32[]{:S(2)}) async-start(bf16[4,2,96,768]{3,2,1,0:T(8,128)(2,1)} %broadcast_in_dim.110), calls=%async_computation.2 | async-start | bytes 2359296 | tf_op jit(solution)/shard_map/all_to_all | solution.py:445
  127.6 5.2 %weight_grads.1 = (bf16[384,768]{1,0:T(8,128)(2,1)}, bf16[384,768]{1,0:T(8,128)(2,1)S(1)}, bf16[640,384]{1,0:T(8,128)(2,1)S(1)}) custom-call(s32[2]{0:T(128)S(1)} %pad_add_fusion.me_ref, f32[960,384]{1,0:T(8,128)} %copy-done.5, bf16[960,384]{1,0:T(8,128)(2,1)} %collective-permute-done.11.k_far, f32[960,384]{1,0:T(8,128)} %copy-done.4, ...), custom_call_target="tpu_custom_call" | custom-call | flops 5500000256 | bytes 15000000 | tf_op jit(solution)/shard_map/weight_grads/pallas_call | solution.py:394
  133.3 1.9 fusion.8
  138.2 1.3 collective-permute-start.16
  139.5 2.4 collective-permute-done.16
  143.0 6.2 %collective-permute-done.18 = bf16[384,768]{1,0:T(8,128)(2,1)} collective-permute-done((bf16[384,768]{1,0:T(8,128)(2,1)}, bf16[384,768]{1,0:T(8,128)(2,1)}, u32[]{:S(2)}, u32[]{:S(2)}) %collective-permute-start.18) | collective-permute-done | bytes 589856 | tf_op jit(solution)/shard_map/ppermute | solution.py:27
  149.2 1.2 add_convert_fusion
  151.2 3.5 %collective-permute-start.22 = (bf16[96,768]{1,0:T(8,128)(2,1)}, bf16[96,768]{1,0:T(8,128)(2,1)S(1)}, u32[]{:S(2)}, u32[]{:S(2)}) collective-permute-start(bf16[96,768]{1,0:T(8,128)(2,1)} %get-tuple-element.185), channel_id=1, source_target_pairs={{0,24},{4,28},{8,16},{12,20},{16,8},{20,12},{24,0},{28,4},{1,25},{... | collective-permute-start | bytes 442376 | tf_op jit(solution)/shard_map/ppermute | solution.py:27
  155.6 1.9 add_convert_fusion.2
  157.6 1.3 collective-permute-start.15
  160.5 3.0 %collective-permute-done.19 = f32[288]{0:T(512)S(1)} collective-permute-done((f32[288]{0:T(512)S(1)}, f32[288]{0:T(512)S(1)}, u32[]{:S(2)}, u32[]{:S(2)}) %collective-permute-start.19) | collective-permute-done | bytes 1184 | tf_op jit(solution)/shard_map/ppermute | solution.py:27
  164.3 5.7 %collective-permute-done.21 = bf16[96,768]{1,0:T(8,128)(2,1)S(1)} collective-permute-done((bf16[96,768]{1,0:T(8,128)(2,1)}, bf16[96,768]{1,0:T(8,128)(2,1)S(1)}, u32[]{:S(2)}, u32[]{:S(2)}) %collective-permute-start.21) | collective-permute-done | bytes 147488 | tf_op jit(solution)/shard_map/ppermute | solution.py:27
  170.2 1.5 collective-permute-start.25
  171.7 2.9 %collective-permute-start.23 = (bf16[1,96,768]{2,1,0:T(8,128)(2,1)S(1)}, bf16[1,96,768]{2,1,0:T(8,128)(2,1)S(1)}, u32[]{:S(2)}, u32[]{:S(2)}) collective-permute-start(bf16[1,96,768]{2,1,0:T(8,128)(2,1)S(1)} %bitcast.117), channel_id=1, source_target_pairs={{0,8},{4,12},{8,0},{12,4},{16,24},{20,28},{24,16},{28,20},{1,9},{5... | collective-permute-start | bytes 442376 | tf_op jit(solution)/shard_map/ppermute | solution.py:27
  174.6 1.5 convert_add_fusion.1
  176.1 1.8 fusion.22
  177.9 2.7 %multiply_reduce_fusion.2 = (f32[160]{0:T(256)S(1)}, f32[160,768]{1,0:T(8,128)}) fusion(f32[640,768]{1,0:T(8,128)} %get-tuple-element.180, f32[768]{0:T(1024)S(1)} %copy-done.38, bf16[160,768]{1,0:T(8,128)(2,1)S(1)} %pad_maximum_fusion.11, bf16[3,768,768]{2,1,0:T(8,128)(2,1)} %convert_element_type.145, f32[2,160,768]{2,1,0:T(8,128)S(1)} %convert_add_fusion.1), kind=kOutput, calls=%fused_computation.75 | convolution fusion | flops 189235040 | bytes 2903680 | tf_op jit(solution)/shard_map/dot_general | solution.py:39
  181.2 3.0 %collective-permute-done.24 = bf16[1,96,768]{2,1,0:T(8,128)(2,1)S(1)} collective-permute-done((bf16[1,96,768]{2,1,0:T(8,128)(2,1)S(1)}, bf16[1,96,768]{2,1,0:T(8,128)(2,1)S(1)}, u32[]{:S(2)}, u32[]{:S(2)}) %collective-permute-start.24) | collective-permute-done | bytes 147488 | tf_op jit(solution)/shard_map/ppermute | solution.py:27
  184.3 7.4 %collective-permute-done.26.over_ref = bf16[4,2,96,768]{3,2,1,0:T(8,128)(2,1)S(1)} collective-permute-done((bf16[4,2,96,768]{3,2,1,0:T(8,128)(2,1)S(1)}, bf16[4,2,96,768]{3,2,1,0:T(8,128)(2,1)S(1)}, u32[]{:S(2)}, u32[]{:S(2)}) %collective-permute-start.26) | collective-permute-done | bytes 1179680 | tf_op jit(solution)/shard_map/ppermute | solution.py:27
  191.7 1.6 collect.2
  193.7 1.3 collective-permute-start.30
  195.0 1.6 collect.3
  196.6 2.1 multiply_reduce_fusion
  200.7 1.4 collective-permute-start.33
  202.1 2.3 collective-permute-done.29
  204.4 3.6 %collective-permute-done.33 = f32[3,768]{1,0:T(4,128)S(1)} collective-permute-done((f32[3,768]{1,0:T(4,128)S(1)}, f32[3,768]{1,0:T(4,128)S(1)}, u32[]{:S(2)}, u32[]{:S(2)}) %collective-permute-start.33) | collective-permute-done | bytes 9248 | tf_op jit(solution)/shard_map/ppermute | solution.py:27
  208.8 1.3 collective-permute-start.31
  210.8 1.5 collective-permute-start.34
  215.1 6.6 %multiply_subtract_fusion = (f32[768,768]{1,0:T(8,128)}, f32[768,768]{1,0:T(8,128)}) fusion(f32[768,768]{1,0:T(8,128)} %param.23, f32[768,768]{1,0:T(8,128)} %get-tuple-element.76, f32[768]{0:T(1024)S(1)} %get-tuple-element.157, f32[768]{0:T(1024)S(1)} %rsqrt.52, f32[768,768]{1,0:T(8,128)} %param.22, f32[768]{0:T(1024)S(1)} %get-tuple-element.162, ...), kind=kLoop, calls=%fused_computation.11 | loop fusion | flops 3538944 | bytes 14168064 | tf_op jit(solution)/shard_map/sub | solution.py:815
  222.4 2.0 add_bitcast_fusion
  225.9 15.9 %attn_update.1 = (f32[3,768,768]{2,1,0:T(8,128)}, f32[3,768,768]{2,1,0:T(8,128)}, f32[3,1,768]{2,1,0:T(1,128)S(1)}, f32[3,1,768]{2,1,0:T(1,128)S(1)}, f32[1,768,...) custom-call(s32[2]{0:T(128)S(1)} %pad_add_fusion.1.me_ref, ...), custom_call_target="tpu_custom_call" | custom-call | flops 15399999488 | bytes 42000000 | tf_op jit(solution)/shard_map/attn_update/pallas_call | solution.py:588
  (242 shorter events, 38.4 us)
Async XLA Ops:
  0.7 10.3 %collective-permute-start = (bf16[160,768]{1,0:T(8,128)(2,1)}, bf16[160,768]{1,0:T(8,128)(2,1)S(1)}, u32[]{:S(2)}, u32[]{:S(2)}) collective-permute-start(bf16[160,768]{1,0:T(8,128)(2,1)} %bitcast.107), channel_id=1, source_target_pairs={{0,2},{1,3},{2,0},{3,1},{4,6},{5,7},{6,4},{7,5},{8,10},{9,11},{10,... | collective-permute-start | bytes 737288 | tf_op jit(solution)/shard_map/ppermute | solution.py:27
  11.0 1.9 collective-permute-start.1
  11.6 19.1 %collective-permute-start.3 = (bf16[160,768]{1,0:T(8,128)(2,1)}, bf16[160,768]{1,0:T(8,128)(2,1)S(1)}, u32[]{:S(2)}, u32[]{:S(2)}) collective-permute-start(bf16[160,768]{1,0:T(8,128)(2,1)} %bitcast.10), channel_id=1, source_target_pairs={{0,2},{1,3},{2,0},{3,1},{4,6},{5,7},{6,4},{7,5},{8,10},{9,11},{10,... | collective-permute-start | bytes 737288 | tf_op jit(solution)/shard_map/ppermute | solution.py:27
  13.3 128.6 %copy-start.40 = (f32[640]{0:T(1024)}, f32[640]{0:T(1024)S(1)}, u32[]{:S(2)}) copy-start(f32[640]{0:T(1024)S(1)} %add_rsqrt_fusion.1) | copy-start | bytes 7684
  18.3 12.5 %copy-start.2 = (bf16[640,768]{1,0:T(8,128)(2,1)}, bf16[640,768]{1,0:T(8,128)(2,1)S(1)}, u32[]{:S(2)}) copy-start(bf16[640,768]{1,0:T(8,128)(2,1)S(1)} %convolution_convert_fusion.4.v_ref) | copy-start | bytes 2949124
  18.3 14.8 %copy-start.16 = (f32[768,768]{1,0:T(8,128)S(1)}, f32[768,768]{1,0:T(8,128)}, u32[]{:S(2)}) copy-start(f32[768,768]{1,0:T(8,128)} %param.20) | copy-start | bytes 7077892
  32.1 1.9 collective-permute-start.4
  32.3 8.2 %collective-permute-start.2 = (bf16[160,768]{1,0:T(8,128)(2,1)S(1)}, bf16[160,768]{1,0:T(8,128)(2,1)S(1)}, u32[]{:S(2)}, u32[]{:S(2)}) collective-permute-start(bf16[160,768]{1,0:T(8,128)(2,1)S(1)} %get-tuple-element.93), channel_id=1, source_target_pairs={{0,2},{1,3},{2,0},{3,1},{4,6},{5,7},{6,4},{7,5},{8,10},{9,11},{10,... | collective-permute-start | bytes 737288 | tf_op jit(solution)/shard_map/ppermute | solution.py:27
  33.7 8.8 %copy-start.13 = (bf16[768,768]{1,0:T(8,128)(2,1)}, bf16[768,768]{1,0:T(8,128)(2,1)S(1)}, u32[]{:S(2)}) copy-start(bf16[768,768]{1,0:T(8,128)(2,1)S(1)} %convert_element_type.153) | copy-start | bytes 3538948
  40.6 1.9 collective-permute-start.5
  43.6 8.1 %copy-start.39 = (f32[640]{0:T(1024)}, f32[640]{0:T(1024)S(1)}, u32[]{:S(2)}) copy-start(f32[640]{0:T(1024)S(1)} %add_rsqrt_fusion) | copy-start | bytes 7684
  51.6 2.7 %collective-permute-start.6 = (bf16[320,768]{1,0:T(8,128)(2,1)}, bf16[320,768]{1,0:T(8,128)(2,1)S(1)}, u32[]{:S(2)}, u32[]{:S(2)}) collective-permute-start(bf16[320,768]{1,0:T(8,128)(2,1)} %pad_maximum_fusion.9), channel_id=1, source_target_pairs={{0,1},{1,0},{2,3},{3,2},{4,5},{5,4},{6,7},{7,6},{8,9},{9,8},{10,11... | collective-permute-start | bytes 1474568 | tf_op jit(solution)/shard_map/ppermute | solution.py:27
  54.3 12.7 %copy-start.23 = (bf16[320,768]{1,0:T(8,128)(2,1)}, bf16[320,768]{1,0:T(8,128)(2,1)S(1)}, u32[]{:S(2)}) copy-start(bf16[320,768]{1,0:T(8,128)(2,1)S(1)} %collective-permute-done.6) | copy-start | bytes 1474564
  56.3 10.7 %collective-permute-start.7 = (bf16[160,768]{1,0:T(8,128)(2,1)}, bf16[160,768]{1,0:T(8,128)(2,1)S(1)}, u32[]{:S(2)}, u32[]{:S(2)}) collective-permute-start(bf16[160,768]{1,0:T(8,128)(2,1)} %fusion.19), channel_id=1, source_target_pairs={{0,2},{1,3},{2,0},{3,1},{4,6},{5,7},{6,4},{7,5},{8,10},{9,11},{10,... | collective-permute-start | bytes 737288 | tf_op jit(solution)/shard_map/ppermute | solution.py:27
  58.2 19.7 %collective-permute-start.8 = (bf16[384,768]{1,0:T(8,128)(2,1)}, bf16[384,768]{1,0:T(8,128)(2,1)}, u32[]{:S(2)}, u32[]{:S(2)}) collective-permute-start(bf16[384,768]{1,0:T(8,128)(2,1)} %get-tuple-element.179), channel_id=1, source_target_pairs={{0,4},{4,0},{8,12},{12,8},{16,20},{20,16},{24,28},{28,24},{1,5},{5... | collective-permute-start | bytes 1769480 | tf_op jit(solution)/shard_map/ppermute | solution.py:27
  61.9 6.7 %slice-start = ((f32[640]{0:T(1024)}), f32[160]{0:T(256)S(1)}, s32[]{:S(2)}) async-start(f32[640]{0:T(1024)} %copy-done.39), calls=%async_computation.3 | async-start | bytes 2048 | tf_op jit(solution)/shard_map/slice | solution.py:737
  61.9 38.2 %all-to-all-start = ((bf16[4,192,768]{2,1,0:T(8,128)(2,1)}), bf16[4,192,768]{2,1,0:T(8,128)(2,1)}, u32[]{:S(2)}, u32[]{:S(2)}) async-start(bf16[4,192,768]{2,1,0:T(8,128)(2,1)} %bitcast.112), calls=%async_computation | async-start | bytes 2359296 | tf_op jit(solution)/shard_map/all_to_all | solution.py:445
  71.6 6.3 %copy-start.17 = (bf16[384,768]{1,0:T(8,128)(2,1)S(1)}, bf16[384,768]{1,0:T(8,128)(2,1)}, u32[]{:S(2)}) copy-start(bf16[384,768]{1,0:T(8,128)(2,1)} %get-tuple-element.104) | copy-start | bytes 1769476
  71.7 8.3 %copy-start.3 = (bf16[640,768]{1,0:T(8,128)(2,1)S(1)}, bf16[640,768]{1,0:T(8,128)(2,1)}, u32[]{:S(2)}) copy-start(bf16[640,768]{1,0:T(8,128)(2,1)} %copy-done.2) | copy-start | bytes 2949124
  75.5 19.3 %collective-permute-start.10 = (bf16[2,800,384]{2,1,0:T(8,128)(2,1)}, bf16[2,800,384]{2,1,0:T(8,128)(2,1)}, u32[]{:S(2)}, u32[]{:S(2)}) collective-permute-start(bf16[2,800,384]{2,1,0:T(8,128)(2,1)} %back_values.1.own_send.own_keep), channel_id=1, source_target_pairs={{0,1},{2,3},{4,5},{6,7},{8,9},{10,11},{12,13},{14,15},{16,17},{18,... | collective-permute-start | bytes 3686408 | tf_op jit(solution)/shard_map/ppermute | solution.py:317
  80.0 13.8 %copy-start.29 = (bf16[160,768]{1,0:T(8,128)(2,1)S(1)}, bf16[160,768]{1,0:T(8,128)(2,1)}, u32[]{:S(2)}) copy-start(bf16[160,768]{1,0:T(8,128)(2,1)} %copy-done.28) | copy-start | bytes 737284
  80.0 13.8 %copy-start.31 = (bf16[160,768]{1,0:T(8,128)(2,1)S(1)}, bf16[160,768]{1,0:T(8,128)(2,1)}, u32[]{:S(2)}) copy-start(bf16[160,768]{1,0:T(8,128)(2,1)} %copy-done.30) | copy-start | bytes 737284
  92.4 14.2 %collective-permute-start.9 = (bf16[2,800,384]{2,1,0:T(8,128)(2,1)}, bf16[2,800,384]{2,1,0:T(8,128)(2,1)}, u32[]{:S(2)}, u32[]{:S(2)}) collective-permute-start(bf16[2,800,384]{2,1,0:T(8,128)(2,1)} %get-tuple-element.106.own_send.own_keep), channel_id=1, source_target_pairs={{1,0},{3,2},{5,4},{7,6},{9,8},{11,10},{13,12},{15,14},{17,16},{19,... | collective-permute-start | bytes 3686408 | tf_op jit(solution)/shard_map/ppermute | solution.py:317
  98.6 29.1 %collective-permute-start.13 = (bf16[960,384]{1,0:T(8,128)(2,1)}, bf16[960,384]{1,0:T(8,128)(2,1)}, u32[]{:S(2)}, u32[]{:S(2)}) collective-permute-start(bf16[960,384]{1,0:T(8,128)(2,1)} %get-tuple-element.108), channel_id=1, source_target_pairs={{1,3},{3,1},{5,7},{7,5},{9,11},{11,9},{13,15},{15,13},{17,19},{19,... | collective-permute-start | bytes 2211848 | tf_op jit(solution)/shard_map/ppermute | solution.py:321
  101.6 21.2 %all-to-all-start.1 = ((bf16[4,96,768]{2,1,0:T(8,128)(2,1)}), bf16[4,96,768]{2,1,0:T(8,128)(2,1)S(1)}, u32[]{:S(2)}, u32[]{:S(2)}) async-start(bf16[4,96,768]{2,1,0:T(8,128)(2,1)} %bitcast.15), calls=%async_computation.1 | async-start | bytes 1179648 | tf_op jit(solution)/shard_map/all_to_all | solution.py:445
  106.6 6.7 %copy-start.19 = (f32[768,768]{1,0:T(8,128)S(1)}, f32[768,768]{1,0:T(8,128)}, u32[]{:S(2)}) copy-start(f32[768,768]{1,0:T(8,128)} %param.23) | copy-start | bytes 7077892
  106.6 6.7 %copy-start.45 = (bf16[640,768]{1,0:T(8,128)(2,1)S(1)}, bf16[640,768]{1,0:T(8,128)(2,1)}, u32[]{:S(2)}) copy-start(bf16[640,768]{1,0:T(8,128)(2,1)} %get-tuple-element.116) | copy-start | bytes 2949124
  109.5 18.2 %collective-permute-start.11 = (bf16[960,384]{1,0:T(8,128)(2,1)}, bf16[960,384]{1,0:T(8,128)(2,1)}, u32[]{:S(2)}, u32[]{:S(2)}) collective-permute-start(bf16[960,384]{1,0:T(8,128)(2,1)} %get-tuple-element.112), channel_id=1, source_target_pairs={{0,2},{2,0},{4,6},{6,4},{8,10},{10,8},{12,14},{14,12},{16,18},{18,... | collective-permute-start | bytes 2211848 | tf_op jit(solution)/shard_map/ppermute | solution.py:321
  112.7 6.2 %collective-permute-start.12 = (bf16[96,768]{1,0:T(8,128)(2,1)S(1)}, bf16[96,768]{1,0:T(8,128)(2,1)S(1)}, u32[]{:S(2)}, u32[]{:S(2)}) collective-permute-start(bf16[96,768]{1,0:T(8,128)(2,1)S(1)} %get-tuple-element.195), channel_id=1, source_target_pairs={{0,4},{4,0},{8,12},{12,8},{16,20},{20,16},{24,28},{28,24},{1,5},{5... | collective-permute-start | bytes 442376 | tf_op jit(solution)/shard_map/ppermute | solution.py:27
  124.1 39.8 %all-to-all-start.2 = ((bf16[4,2,96,768]{3,2,1,0:T(8,128)(2,1)}), bf16[4,2,96,768]{3,2,1,0:T(8,128)(2,1)S(1)}, u32[]{:S(2)}, u32[]{:S(2)}) async-start(bf16[4,2,96,768]{3,2,1,0:T(8,128)(2,1)} %broadcast_in_dim.110), calls=%async_computation.2 | async-start | bytes 2359296 | tf_op jit(solution)/shard_map/all_to_all | solution.py:445
  132.8 16.4 %collective-permute-start.18 = (bf16[384,768]{1,0:T(8,128)(2,1)}, bf16[384,768]{1,0:T(8,128)(2,1)}, u32[]{:S(2)}, u32[]{:S(2)}) collective-permute-start(bf16[384,768]{1,0:T(8,128)(2,1)} %get-tuple-element.126), channel_id=1, source_target_pairs={{0,4},{4,0},{8,12},{12,8},{16,20},{20,16},{24,28},{28,24},{1,5},{5... | collective-permute-start | bytes 1769480 | tf_op jit(solution)/shard_map/ppermute | solution.py:27
  135.4 13.9 %copy-start.1 = (bf16[384,768]{1,0:T(8,128)(2,1)S(1)}, bf16[384,768]{1,0:T(8,128)(2,1)}, u32[]{:S(2)}) copy-start(bf16[384,768]{1,0:T(8,128)(2,1)} %copy-done) | copy-start | bytes 1769476
  136.4 19.2 %collective-permute-start.14 = (bf16[2,320,768]{2,1,0:T(8,128)(2,1)}, bf16[2,320,768]{2,1,0:T(8,128)(2,1)}, u32[]{:S(2)}, u32[]{:S(2)}) collective-permute-start(bf16[2,320,768]{2,1,0:T(8,128)(2,1)} %pad_maximum_fusion.3), channel_id=1, source_target_pairs={{0,1},{1,0},{2,3},{3,2},{4,5},{5,4},{6,7},{7,6},{8,9},{9,8},{10,11... | collective-permute-start | bytes 2949128 | tf_op jit(solution)/shard_map/ppermute | solution.py:27
  138.2 3.7 %collective-permute-start.16 = (f32[288]{0:T(512)S(1)}, f32[288]{0:T(512)S(1)}, u32[]{:S(2)}, u32[]{:S(2)}) collective-permute-start(f32[288]{0:T(512)S(1)} %reshape.263), channel_id=1, source_target_pairs={{0,2},{1,3},{2,0},{3,1},{4,6},{5,7},{6,4},{7,5},{8,10},{9,11},{10,... | collective-permute-start | bytes 3464 | tf_op jit(solution)/shard_map/ppermute | solution.py:27
  141.9 1.2 collective-permute-start.17
  141.9 13.8 %copy-start.11 = (bf16[640,768]{1,0:T(8,128)(2,1)S(1)}, bf16[640,768]{1,0:T(8,128)(2,1)}, u32[]{:S(2)}) copy-start(bf16[640,768]{1,0:T(8,128)(2,1)} %convolution_convert_fusion.3) | copy-start | bytes 2949124
  151.2 13.1 %collective-permute-start.22 = (bf16[96,768]{1,0:T(8,128)(2,1)}, bf16[96,768]{1,0:T(8,128)(2,1)S(1)}, u32[]{:S(2)}, u32[]{:S(2)}) collective-permute-start(bf16[96,768]{1,0:T(8,128)(2,1)} %get-tuple-element.185), channel_id=1, source_target_pairs={{0,24},{4,28},{8,16},{12,20},{16,8},{20,12},{24,0},{28,4},{1,25},{... | collective-permute-start | bytes 442376 | tf_op jit(solution)/shard_map/ppermute | solution.py:27
  154.7 15.3 %collective-permute-start.21 = (bf16[96,768]{1,0:T(8,128)(2,1)}, bf16[96,768]{1,0:T(8,128)(2,1)S(1)}, u32[]{:S(2)}, u32[]{:S(2)}) collective-permute-start(bf16[96,768]{1,0:T(8,128)(2,1)} %get-tuple-element.186), channel_id=1, source_target_pairs={{0,16},{4,20},{8,24},{12,28},{16,0},{20,4},{24,8},{28,12},{1,17},{... | collective-permute-start | bytes 442376 | tf_op jit(solution)/shard_map/ppermute | solution.py:27
  154.7 15.3 %collective-permute-start.20 = (bf16[96,768]{1,0:T(8,128)(2,1)}, bf16[96,768]{1,0:T(8,128)(2,1)S(1)}, u32[]{:S(2)}, u32[]{:S(2)}) collective-permute-start(bf16[96,768]{1,0:T(8,128)(2,1)} %get-tuple-element.187), channel_id=1, source_target_pairs={{0,8},{4,12},{8,0},{12,4},{16,24},{20,28},{24,16},{28,20},{1,9},{5... | collective-permute-start | bytes 442376 | tf_op jit(solution)/shard_map/ppermute | solution.py:27
  157.6 17.1 %collective-permute-start.15 = (bf16[2,160,768]{2,1,0:T(8,128)(2,1)}, bf16[2,160,768]{2,1,0:T(8,128)(2,1)}, u32[]{:S(2)}, u32[]{:S(2)}) collective-permute-start(bf16[2,160,768]{2,1,0:T(8,128)(2,1)} %add_convert_fusion.2), channel_id=1, source_target_pairs={{0,2},{1,3},{2,0},{3,1},{4,6},{5,7},{6,4},{7,5},{8,10},{9,11},{10,... | collective-permute-start | bytes 1474568 | tf_op jit(solution)/shard_map/ppermute | solution.py:27
  159.8 3.7 %collective-permute-start.19 = (f32[288]{0:T(512)S(1)}, f32[288]{0:T(512)S(1)}, u32[]{:S(2)}, u32[]{:S(2)}) collective-permute-start(f32[288]{0:T(512)S(1)} %add.247), channel_id=1, source_target_pairs={{0,4},{4,0},{8,12},{12,8},{16,20},{20,16},{24,28},{28,24},{1,5},{5... | collective-permute-start | bytes 3464 | tf_op jit(solution)/shard_map/ppermute | solution.py:27
  163.8 27.8 %collective-permute-start.26 = (bf16[4,2,96,768]{3,2,1,0:T(8,128)(2,1)S(1)}, bf16[4,2,96,768]{3,2,1,0:T(8,128)(2,1)S(1)}, u32[]{:S(2)}, u32[]{:S(2)}) collective-permute-start(bf16[4,2,96,768]{3,2,1,0:T(8,128)(2,1)S(1)} %all-to-all-done.2.own_ref), channel_id=1, source_target_pairs={{0,4},{4,0},{8,12},{12,8},{16,20},{20,16},{24,28},{28,24},{1,5},{5... | collective-permute-start | bytes 3538952 | tf_op jit(solution)/shard_map/ppermute | solution.py:27
  170.2 11.0 %collective-permute-start.25 = (bf16[1,96,768]{2,1,0:T(8,128)(2,1)S(1)}, bf16[1,96,768]{2,1,0:T(8,128)(2,1)S(1)}, u32[]{:S(2)}, u32[]{:S(2)}) collective-permute-start(bf16[1,96,768]{2,1,0:T(8,128)(2,1)S(1)} %bitcast.115), channel_id=1, source_target_pairs={{0,24},{4,28},{8,16},{12,20},{16,8},{20,12},{24,0},{28,4},{1,25},{... | collective-permute-start | bytes 442376 | tf_op jit(solution)/shard_map/ppermute | solution.py:27
  171.7 12.5 %collective-permute-start.24 = (bf16[1,96,768]{2,1,0:T(8,128)(2,1)S(1)}, bf16[1,96,768]{2,1,0:T(8,128)(2,1)S(1)}, u32[]{:S(2)}, u32[]{:S(2)}) collective-permute-start(bf16[1,96,768]{2,1,0:T(8,128)(2,1)S(1)} %bitcast.116), channel_id=1, source_target_pairs={{0,16},{4,20},{8,24},{12,28},{16,0},{20,4},{24,8},{28,12},{1,17},{... | collective-permute-start | bytes 442376 | tf_op jit(solution)/shard_map/ppermute | solution.py:27
  171.7 12.5 %collective-permute-start.23 = (bf16[1,96,768]{2,1,0:T(8,128)(2,1)S(1)}, bf16[1,96,768]{2,1,0:T(8,128)(2,1)S(1)}, u32[]{:S(2)}, u32[]{:S(2)}) collective-permute-start(bf16[1,96,768]{2,1,0:T(8,128)(2,1)S(1)} %bitcast.117), channel_id=1, source_target_pairs={{0,8},{4,12},{8,0},{12,4},{16,24},{20,28},{24,16},{28,20},{1,9},{5... | collective-permute-start | bytes 442376 | tf_op jit(solution)/shard_map/ppermute | solution.py:27
  193.2 14.8 %collective-permute-start.27 = (bf16[4,96,768]{2,1,0:T(8,128)(2,1)S(1)}, bf16[4,96,768]{2,1,0:T(8,128)(2,1)S(1)}, u32[]{:S(2)}, u32[]{:S(2)}) collective-permute-start(bf16[4,96,768]{2,1,0:T(8,128)(2,1)S(1)} %pad_maximum_fusion.4.refs_0_), channel_id=1, source_target_pairs={{0,4},{4,0},{8,12},{12,8},{16,20},{20,16},{24,28},{28,24},{1,5},{5... | collective-permute-start | bytes 1769480 | tf_op jit(solution)/shard_map/ppermute | solution.py:27
  193.7 16.4 %collective-permute-start.30 = (bf16[4,96,768]{2,1,0:T(8,128)(2,1)S(1)}, bf16[4,96,768]{2,1,0:T(8,128)(2,1)S(1)}, u32[]{:S(2)}, u32[]{:S(2)}) collective-permute-start(bf16[4,96,768]{2,1,0:T(8,128)(2,1)S(1)} %pad_maximum_fusion.4.refs_0_), channel_id=1, source_target_pairs={{0,2},{1,3},{2,0},{3,1},{4,6},{5,7},{6,4},{7,5},{8,10},{9,11},{10,... | collective-permute-start | bytes 1769480 | tf_op jit(solution)/shard_map/ppermute | solution.py:27
  195.0 30.8 %collective-permute-start.35 = (bf16[4,96,768]{2,1,0:T(8,128)(2,1)S(1)}, bf16[4,96,768]{2,1,0:T(8,128)(2,1)S(1)}, u32[]{:S(2)}, u32[]{:S(2)}) collective-permute-start(bf16[4,96,768]{2,1,0:T(8,128)(2,1)S(1)} %pad_maximum_fusion.4.refs_0_), channel_id=1, source_target_pairs={{0,1},{1,0},{2,3},{3,2},{4,5},{5,4},{6,7},{7,6},{8,9},{9,8},{10,11... | collective-permute-start | bytes 1769480 | tf_op jit(solution)/shard_map/ppermute | solution.py:27
  195.0 4.9 %collective-permute-start.28 = (f32[288]{0:T(512)S(1)}, f32[288]{0:T(512)S(1)}, u32[]{:S(2)}, u32[]{:S(2)}) collective-permute-start(f32[288]{0:T(512)S(1)} %add.253), channel_id=1, source_target_pairs={{0,8},{4,12},{8,0},{12,4},{16,24},{20,28},{24,16},{28,20},{1,9},{5... | collective-permute-start | bytes 3464 | tf_op jit(solution)/shard_map/ppermute | solution.py:27
  198.8 1.9 collective-permute-start.32
  199.9 4.5 %collective-permute-start.29 = (f32[288]{0:T(512)S(1)}, f32[288]{0:T(512)S(1)}, u32[]{:S(2)}, u32[]{:S(2)}) collective-permute-start(f32[288]{0:T(512)S(1)} %add.273), channel_id=1, source_target_pairs={{0,16},{4,20},{8,24},{12,28},{16,0},{20,4},{24,8},{28,12},{1,17},{... | collective-permute-start | bytes 3464 | tf_op jit(solution)/shard_map/ppermute | solution.py:27
  200.7 7.3 %collective-permute-start.33 = (f32[3,768]{1,0:T(4,128)S(1)}, f32[3,768]{1,0:T(4,128)S(1)}, u32[]{:S(2)}, u32[]{:S(2)}) collective-permute-start(f32[3,768]{1,0:T(4,128)S(1)} %fusion.35), channel_id=1, source_target_pairs={{0,2},{1,3},{2,0},{3,1},{4,6},{5,7},{6,4},{7,5},{8,10},{9,11},{10,... | collective-permute-start | bytes 27656 | tf_op jit(solution)/shard_map/ppermute | solution.py:27
  202.1 19.7 %copy-start.41 = (f32[768]{0:T(1024)}, f32[768]{0:T(1024)S(1)}, u32[]{:S(2)}) copy-start(f32[768]{0:T(1024)S(1)} %multiply_reduce_fusion.5) | copy-start | bytes 9220
  208.8 17.0 %collective-permute-start.36 = (bf16[4,96,768]{2,1,0:T(8,128)(2,1)S(1)}, bf16[4,96,768]{2,1,0:T(8,128)(2,1)S(1)}, u32[]{:S(2)}, u32[]{:S(2)}) collective-permute-start(bf16[4,96,768]{2,1,0:T(8,128)(2,1)S(1)} %collective-permute-done.27.refs_1_), channel_id=1, source_target_pairs={{0,1},{1,0},{2,3},{3,2},{4,5},{5,4},{6,7},{7,6},{8,9},{9,8},{10,11... | collective-permute-start | bytes 1769480 | tf_op jit(solution)/shard_map/ppermute | solution.py:27
  208.8 13.0 %collective-permute-start.31 = (bf16[2,96,768]{2,1,0:T(8,128)(2,1)}, bf16[2,96,768]{2,1,0:T(8,128)(2,1)S(1)}, u32[]{:S(2)}, u32[]{:S(2)}) collective-permute-start(bf16[2,96,768]{2,1,0:T(8,128)(2,1)} %slice.177), channel_id=1, source_target_pairs={{0,2},{1,3},{2,0},{3,1},{4,6},{5,7},{6,4},{7,5},{8,10},{9,11},{10,... | collective-permute-start | bytes 884744 | tf_op jit(solution)/shard_map/ppermute | solution.py:27
  210.8 10.9 %collective-permute-start.34 = (bf16[2,96,768]{2,1,0:T(8,128)(2,1)}, bf16[2,96,768]{2,1,0:T(8,128)(2,1)}, u32[]{:S(2)}, u32[]{:S(2)}) collective-permute-start(bf16[2,96,768]{2,1,0:T(8,128)(2,1)} %slice.214), channel_id=1, source_target_pairs={{0,4},{4,0},{8,12},{12,8},{16,20},{20,16},{24,28},{28,24},{1,5},{5... | collective-permute-start | bytes 884744 | tf_op jit(solution)/shard_map/ppermute | solution.py:27
  214.3 7.4 %copy-start.42 = (f32[768]{0:T(1024)}, f32[768]{0:T(1024)S(1)}, u32[]{:S(2)}) copy-start(f32[768]{0:T(1024)S(1)} %get-tuple-element.160) | copy-start | bytes 9220
  215.0 10.9 %collective-permute-start.37 = (bf16[4,96,768]{2,1,0:T(8,128)(2,1)S(1)}, bf16[4,96,768]{2,1,0:T(8,128)(2,1)}, u32[]{:S(2)}, u32[]{:S(2)}) collective-permute-start(bf16[4,96,768]{2,1,0:T(8,128)(2,1)S(1)} %collective-permute-done.30.refs_2_), channel_id=1, source_target_pairs={{0,1},{1,0},{2,3},{3,2},{4,5},{5,4},{6,7},{7,6},{8,9},{9,8},{10,11... | collective-permute-start | bytes 1769480 | tf_op jit(solution)/shard_map/ppermute | solution.py:27
  215.1 7.3 %copy-start.21 = (f32[160,768]{1,0:T(8,128)S(1)}, f32[160,768]{1,0:T(8,128)}, u32[]{:S(2)}) copy-start(f32[160,768]{1,0:T(8,128)} %get-tuple-element.167) | copy-start | bytes 1474564
  215.1 7.3 %copy-start.22 = (f32[160,768]{1,0:T(8,128)S(1)}, f32[160,768]{1,0:T(8,128)}, u32[]{:S(2)}) copy-start(f32[160,768]{1,0:T(8,128)} %get-tuple-element.203) | copy-start | bytes 1474564
  215.1 7.3 %slice-start.1 = ((f32[640]{0:T(1024)}), f32[160]{0:T(256)S(1)}, s32[]{:S(2)}) async-start(f32[640]{0:T(1024)} %copy-done.40), calls=%async_computation.4 | async-start | bytes 2048 | tf_op jit(solution)/shard_map/slice | solution.py:692
  215.1 7.3 %copy-start.44 = (f32[160]{0:T(256)S(1)}, f32[160]{0:T(256)}, u32[]{:S(2)}) copy-start(f32[160]{0:T(256)} %broadcast_multiply_fusion.1) | copy-start | bytes 1924
  221.8 4.0 %collective-permute-start.38 = (bf16[2,96,768]{2,1,0:T(8,128)(2,1)S(1)}, bf16[2,96,768]{2,1,0:T(8,128)(2,1)}, u32[]{:S(2)}, u32[]{:S(2)}) collective-permute-start(bf16[2,96,768]{2,1,0:T(8,128)(2,1)S(1)} %collective-permute-done.31.refs_3_), channel_id=1, source_target_pairs={{0,1},{1,0},{2,3},{3,2},{4,5},{5,4},{6,7},{7,6},{8,9},{9,8},{10,11... | collective-permute-start | bytes 884744 | tf_op jit(solution)/shard_map/ppermute | solution.py:27
  222.3 3.5 %collective-permute-start.39 = (bf16[2,96,768]{2,1,0:T(8,128)(2,1)}, bf16[2,96,768]{2,1,0:T(8,128)(2,1)}, u32[]{:S(2)}, u32[]{:S(2)}) collective-permute-start(bf16[2,96,768]{2,1,0:T(8,128)(2,1)} %collective-permute-done.34.refs_4_), channel_id=1, source_target_pairs={{0,1},{1,0},{2,3},{3,2},{4,5},{5,4},{6,7},{7,6},{8,9},{9,8},{10,11... | collective-permute-start | bytes 884744 | tf_op jit(solution)/shard_map/ppermute | solution.py:27
  (27 other events, 82.4 us)
